TPU v7x, 512 devices: a whole 4x4x16 slice. The times are simulated.
512 devices in a mesh: lat: 16 (over x, z_hi, core), lon: 32 (over z_lo, y).
Axes of the slice: x: 4, y: 4, z: 16 (z_hi: 2, z_lo: 8; z = z_hi * 8 + z_lo), core: 2. Of those that a mesh axis runs over, the one named last changes fastest.
Arguments:
- prior_ensemble: bfloat16 [3, 128, 32, 4096], P(None, None, 'lat', 'lon'), may hold values from -6 to 6
- observed: float32 [16, 32, 256], P('lat', 'lon'), may hold values from -6 to 6
- obs_error: float32 [16, 32, 256], P('lat', 'lon'), may hold values from 0.2 to 80
- obs_index: int32 [16, 32, 256], P('lat', 'lon'), may hold values from 0 to 767
- obs_count: int32 [16, 32], P('lat', 'lon'), may hold values from 128 to 256, as said below
Outputs:
- posterior_ensemble: float32 [3, 128, 32, 4096], P(None, None, 'lat', 'lon')
Inputs may be any that keep to these rules, and one draw needn't show every extreme that they name: `obs_count`: every tile has between 128 and 256 live slots; some tile has all 256.
All inputs are finite; a program needn't handle non-finite values.
Results may differ from a plain program's by a relative error of at most 0.0003.
Values sent between devices are 32-bit elements; how exact they have to be, the bound alone decides.
No kernel may reach another device: no remote copies, remote signals or barrier semaphores. Data moves between devices by JAX's collectives and lax.ppermute only.
A program may use at most 128 MiB of HBM per device.

v0:
```python
import math

import jax
import jax.numpy as jnp
from jax import lax
from jax.sharding import PartitionSpec as P

HALF_COURANT = 0.4
ROTATION = 0.8
BAND = math.pi / 6.0


def with_halo(block, sides, width, periodic):
    for axis, dim in sides:
        count = lax.axis_size(axis)
        forward = [(i, i + 1) for i in range(count - 1)]
        if periodic:
            forward.append((count - 1, 0))
        backward = [(target, source) for source, target in forward]
        low = lax.ppermute(
            lax.slice_in_dim(block, block.shape[dim] - width, None, axis=dim), axis, forward
        )
        high = lax.ppermute(lax.slice_in_dim(block, 0, width, axis=dim), axis, backward)
        block = jnp.concatenate([low, block, high], axis=dim)
    return block


def rotation_rows(first_row, count, total_rows):
    rows = first_row + jnp.arange(count, dtype=jnp.int32)
    latitude = BAND * (2.0 * (rows.astype(jnp.float32) + 0.5) / total_rows - 1.0)
    return (ROTATION * jnp.sin(latitude))[:, None]


def tendency(padded, rotation):
    height, zonal_wind, merid_wind = (padded[0], padded[1], padded[2])
    d_height = -HALF_COURANT * (
        zonal_wind[..., 1:-1, 2:]
        - zonal_wind[..., 1:-1, :-2]
        + (merid_wind[..., 2:, 1:-1] - merid_wind[..., :-2, 1:-1])
    )
    d_zonal = (
        -HALF_COURANT * (height[..., 1:-1, 2:] - height[..., 1:-1, :-2])
        + rotation * merid_wind[..., 1:-1, 1:-1]
    )
    d_merid = (
        -HALF_COURANT * (height[..., 2:, 1:-1] - height[..., :-2, 1:-1])
        - rotation * zonal_wind[..., 1:-1, 1:-1]
    )
    return jnp.stack([d_height, d_zonal, d_merid], axis=0)


def shards(prior_ensemble, observed, obs_error, obs_index, obs_count):
    system_vector = prior_ensemble.astype(jnp.float32)
    ensemble_vectors = system_vector.shape[1]
    lat_rows = system_vector.shape[2]
    lon_cols = system_vector.shape[3]
    total_rows = lat_rows * lax.axis_size("lat")
    first_row = lax.axis_index("lat") * lat_rows
    inner_rotation = rotation_rows(first_row, lat_rows, total_rows)
    padded = with_halo(system_vector, (("lat", 2),), 2, False)
    padded = with_halo(padded, (("lon", 3),), 2, True)
    outer_rotation = rotation_rows(first_row - 1, lat_rows + 2, total_rows)
    wide_rate = tendency(padded, outer_rotation)
    outer_rows = first_row - 1 + jnp.arange(lat_rows + 2, dtype=jnp.int32)
    inside = ((outer_rows >= 0) & (outer_rows < total_rows)).astype(jnp.float32)[:, None]
    wide_mid = (padded[:, :, 1:-1, 1:-1] + wide_rate) * inside
    upper_coefficient = wide_rate[:, :, 1:-1, 1:-1]
    lower_coefficient = tendency(wide_mid, inner_rotation)
    predicted_ensemble = system_vector + 0.5 * (upper_coefficient + lower_coefficient)
    mesh_points = lat_rows * lon_cols
    unrolled_vector = predicted_ensemble.reshape(3, ensemble_vectors, mesh_points)
    index_list = obs_index.reshape(-1)
    slot_total = index_list.shape[0]
    variable_slot = index_list // mesh_points
    cell_index = index_list % mesh_points
    measured_vector = unrolled_vector[variable_slot, :, cell_index]
    state_mean = jnp.mean(measured_vector, axis=-1)
    live = (jnp.arange(slot_total, dtype=jnp.int32) < obs_count.reshape(())).astype(jnp.float32)
    weight_rows = live / obs_error.reshape(-1)
    scaled = (measured_vector - state_mean[:, None]) * weight_rows[:, None]
    innovation = (observed.reshape(-1) - state_mean) * weight_rows
    local_gram = jnp.dot(scaled.T, scaled, precision=lax.Precision.HIGHEST)
    local_push = jnp.dot(innovation, scaled, precision=lax.Precision.HIGHEST)
    identity = jnp.eye(ensemble_vectors, dtype=jnp.float32)
    prior = float(ensemble_vectors - 1)
    gram, push = lax.psum((local_gram, local_push), ("lat", "lon"))
    factor = jnp.linalg.cholesky(prior * identity + gram)
    inverse = lax.linalg.triangular_solve(factor, identity, left_side=True, lower=True)
    transform = math.sqrt(prior) * inverse.T
    forward = lax.linalg.triangular_solve(factor, push[:, None], left_side=True, lower=True)
    mean_weights = lax.linalg.triangular_solve(
        factor, forward, left_side=True, lower=True, transpose_a=True
    )
    weights = transform + mean_weights
    state_center = jnp.mean(unrolled_vector, axis=1, keepdims=True)
    anomaly = unrolled_vector - state_center
    posterior_ensemble = state_center + jnp.einsum(
        "fic,ij->fjc", anomaly, weights, precision=lax.Precision.HIGHEST
    )
    return posterior_ensemble.reshape(predicted_ensemble.shape)


def solution(mesh):
    placed = (
        P(None, None, "lat", "lon"),
        P("lat", "lon", None),
        P("lat", "lon", None),
        P("lat", "lon", None),
        P("lat", "lon"),
    )
    return jax.shard_map(
        shards, mesh=mesh, in_specs=placed, out_specs=P(None, None, "lat", "lon"), check_vma=False
    )
```

profile of v0, /device:TPU:1, one launch (start us, length us, event | category | flops | bytes accessed | tf_op | source)
XLA Modules:
  0.0 556.1 jit_solution(11507215651863218857)
XLA Ops:
  6.5 0.0 all-reduce.2.cloned.1.call-start
  6.5 1.1 copy.12
  7.7 16.8 %collective-permute-start = (f32[3,128,2,128]{1,3,2,0:T(8,128)S(1)}, f32[3,128,2,128]{1,3,2,0:T(8,128)S(1)}, u32[]{:S(2)}, u32[]{:S(2)}) collective-permute-start(f32[3,128,2,128]{1,3,2,0:T(8,128)S(1)} %convert_element_type.32), channel_id=1, source_target_pairs={{0,32},{32,64},{64,96},{96,128},{128,160},{160,192},{192,224},{224... | collective-permute-start | bytes 1179656 | tf_op jit(solution)/shard_map/ppermute | solution.py:20
  24.5 1.9 collective-permute-start.1
  26.5 0.7 fusion.39
  27.2 11.2 %collective-permute-done = f32[3,128,2,128]{1,3,2,0:T(8,128)S(1)} collective-permute-done((f32[3,128,2,128]{1,3,2,0:T(8,128)S(1)}, f32[3,128,2,128]{1,3,2,0:T(8,128)S(1)}, u32[]{:S(2)}, u32[]{:S(2)}) %collective-permute-start) | collective-permute-done | bytes 393248 | tf_op jit(solution)/shard_map/ppermute | solution.py:20
  38.4 12.9 %collective-permute-done.1 = f32[3,128,2,128]{1,3,2,0:T(8,128)S(1)} collective-permute-done((f32[3,128,2,128]{1,3,2,0:T(8,128)S(1)}, f32[3,128,2,128]{1,3,2,0:T(8,128)S(1)}, u32[]{:S(2)}, u32[]{:S(2)}) %collective-permute-start.1) | collective-permute-done | bytes 393248 | tf_op jit(solution)/shard_map/ppermute | solution.py:23
  51.3 3.2 collective-permute-start.2
  54.5 10.8 %collective-permute-start.3 = (f32[3,128,6,2]{1,3,2,0:T(2,128)S(1)}, f32[3,128,6,2]{1,3,2,0:T(2,128)S(1)}, u32[]{:S(2)}, u32[]{:S(2)}) collective-permute-start(f32[3,128,6,2]{1,3,2,0:T(2,128)S(1)} %get-tuple-element.13), channel_id=1, source_target_pairs={{1,0},{2,1},{3,2},{4,3},{5,4},{6,5},{7,6},{8,7},{9,8},{10,9},{11,1... | collective-permute-start | bytes 55304 | tf_op jit(solution)/shard_map/ppermute | solution.py:23
  66.0 0.0 collective-permute-done.2
  66.0 0.2 collective-permute-done.3
  66.1 0.1 pad_maximum_fusion
  66.3 0.1 slice_bitcast_fusion.1
  66.4 0.2 fusion.11
  66.6 0.2 pad_maximum_fusion.1
  66.8 0.1 slice_bitcast_fusion.4
  66.8 0.1 fusion.21
  67.0 0.0 copy-start
  67.0 0.0 copy-start.1
  67.0 0.2 fusion.43
  67.2 1.9 gather_fusion
  69.1 0.1 reduce_sum.19
  69.2 0.0 copy-done
  69.2 0.0 copy-done.1
  69.3 1.2 fusion.26
  70.4 0.0 all-reduce.2.cloned.1.call-update
  70.5 0.3 convolution_bitcast_fusion.2
  70.8 118.6 %psum.15 = f32[128]{0:T(128)S(1)} all-reduce(f32[128]{0:T(128)S(1)} %convolution_bitcast_fusion.2), channel_id=1, replica_groups=mesh['lat'=16,'lon'=32] {'lat','lon'}, use_global_device_ids=true, to_apply=%region_5.6 | all-reduce | flops 128 | bytes 1024 | tf_op jit(solution)/shard_map/psum | solution.py:86
  189.4 333.0 %all-reduce.2.cloned.1.call-done = f32[128,128]{1,0:T(8,128)} async-done(((f32[128,128]{1,0:T(8,128)}), f32[128,128]{1,0:T(8,128)}) %all-reduce.2.cloned.1.call-update) | async-done | bytes 65552 | tf_op jit(solution)/shard_map/psum | solution.py:86
  522.3 0.9 select_add_fusion
  523.2 0.1 copy.13
  523.3 0.9 fusion.31
  524.2 11.7 %cholesky.13 = f32[128,128]{1,0:T(8,128)S(1)} custom-call(f32[128,128]{1,0:T(8,128)S(1)} %fusion.31), custom_call_target="Cholesky" | custom-call | tf_op jit(solution)/shard_map/jit(cholesky)/cholesky | solution.py:87
  535.9 0.6 compare_reduce_fusion
  536.5 0.7 fusion.27
  537.2 9.8 %custom-call.10 = f32[1,128,128]{1,2,0:T(8,128)S(1)} custom-call(f32[1,128,128]{2,1,0:T(8,128)S(1)} %fusion.27), custom_call_target="InvertDiagBlocksLowerTriangular" | custom-call | tf_op jit(solution)/shard_map/triangular_solve | solution.py:88
  547.0 0.2 convolution_bitcast_fusion.1
  547.2 0.2 convolution_bitcast_fusion
  547.4 0.3 fusion.2
  547.7 0.7 fusion
  548.3 0.9 reshape.216
  (9 shorter events, 0.2 us)
Async XLA Ops:
  6.5 515.8 %all-reduce.2.cloned.1.call-start = ((), (), s32[]{:S(2)}) async-start(), calls=%async_computation | async-start | bytes 131072 | tf_op jit(solution)/shard_map/psum | solution.py:86
  7.7 30.7 %collective-permute-start = (f32[3,128,2,128]{1,3,2,0:T(8,128)S(1)}, f32[3,128,2,128]{1,3,2,0:T(8,128)S(1)}, u32[]{:S(2)}, u32[]{:S(2)}) collective-permute-start(f32[3,128,2,128]{1,3,2,0:T(8,128)S(1)} %convert_element_type.32), channel_id=1, source_target_pairs={{0,32},{32,64},{64,96},{96,128},{128,160},{160,192},{192,224},{224... | collective-permute-start | bytes 1179656 | tf_op jit(solution)/shard_map/ppermute | solution.py:20
  24.5 26.7 %collective-permute-start.1 = (f32[3,128,2,128]{1,3,2,0:T(8,128)S(1)}, f32[3,128,2,128]{1,3,2,0:T(8,128)S(1)}, u32[]{:S(2)}, u32[]{:S(2)}) collective-permute-start(f32[3,128,2,128]{1,3,2,0:T(8,128)S(1)} %convert_element_type.32), channel_id=1, source_target_pairs={{32,0},{64,32},{96,64},{128,96},{160,128},{192,160},{224,192},{256... | collective-permute-start | bytes 1179656 | tf_op jit(solution)/shard_map/ppermute | solution.py:23
  51.3 14.7 %collective-permute-start.2 = (f32[3,128,6,2]{1,3,2,0:T(2,128)S(1)}, f32[3,128,6,2]{1,3,2,0:T(2,128)S(1)}, u32[]{:S(2)}, u32[]{:S(2)}) collective-permute-start(f32[3,128,6,2]{1,3,2,0:T(2,128)S(1)} %get-tuple-element.12), channel_id=1, source_target_pairs={{0,1},{1,2},{2,3},{3,4},{4,5},{5,6},{6,7},{7,8},{8,9},{9,10},{10,1... | collective-permute-start | bytes 55304 | tf_op jit(solution)/shard_map/ppermute | solution.py:20
  54.5 11.7 %collective-permute-start.3 = (f32[3,128,6,2]{1,3,2,0:T(2,128)S(1)}, f32[3,128,6,2]{1,3,2,0:T(2,128)S(1)}, u32[]{:S(2)}, u32[]{:S(2)}) collective-permute-start(f32[3,128,6,2]{1,3,2,0:T(2,128)S(1)} %get-tuple-element.13), channel_id=1, source_target_pairs={{1,0},{2,1},{3,2},{4,3},{5,4},{6,5},{7,6},{8,7},{9,8},{10,9},{11,1... | collective-permute-start | bytes 55304 | tf_op jit(solution)/shard_map/ppermute | solution.py:23
  67.0 2.3 copy-start
  67.0 2.2 copy-start.1
Sparse Core Ops, SparseCore 0:
  70.6 451.7 all-reduce.1
where the time goes:
time: 557 us; the launch traced here: 556 us
  waiting for transfers between devices  357 us (64%)
  blocking collectives  119 us (21%)
  starting transfers between devices  32.8 us (6%)
  other arithmetic  26.4 us (5%)
  between operations  14.3 us (3%)
    psum x1, waiting for transfers between devices, shards(): gram, push = lax.psum((local_gram, local_push), ('lat', 'lon'))  333 us
    psum x1, blocking collectives, shards(): gram, push = lax.psum((local_gram, local_push), ('lat', 'lon'))  119 us
    ppermute x2, starting transfers between devices, with_halo(): lax.ppermute(lax.slice_in_dim(block, block.shape[dim] - width, None, axis...  20 us
    ppermute x2, waiting for transfers between devices, with_halo(): lax.ppermute(lax.slice_in_dim(block, 0, width, axis=dim), axis, backward)  13 us
    ppermute x2, starting transfers between devices, with_halo(): lax.ppermute(lax.slice_in_dim(block, 0, width, axis=dim), axis, backward)  12.7 us
    another operation x3, other arithmetic, shards(): factor = jnp.linalg.cholesky(prior * identity + gram)  12.4 us
    ppermute x2, waiting for transfers between devices, with_halo(): lax.ppermute(lax.slice_in_dim(block, block.shape[dim] - width, None, axis...  11.2 us
  transfers between devices with their start and end apart: 5, of which 4 were waited for; matrix products, arithmetic and copies ran while one was open for 0% of the time, Pallas kernels for 0%

commit v1 on v0

v1 whole, which is shorter than its diff:
```python
import math

import jax
import jax.numpy as jnp
from jax import lax
from jax.sharding import Mesh, PartitionSpec as P

HALF_COURANT = 0.4
ROTATION = 0.8
BAND = math.pi / 6.0
LAT = ("x", "zh", "core")
LON = ("zl", "y")
PLANE = ("x", "core", "y")
LINE = ("zh", "zl")


def rotation_at(rows, total_rows):
    latitude = BAND * (2.0 * (rows.astype(jnp.float32) + 0.5) / total_rows - 1.0)
    return ROTATION * jnp.sin(latitude)


def pair_perms(count, periodic):
    inner = [(i, i ^ 1) for i in range(count)]
    outer = []
    for i in range(1, count, 2):
        if i + 1 < count or periodic:
            j = (i + 1) % count
            outer += [(i, j), (j, i)]
    return inner, outer


def swap(low, high, index, axis, perms):
    even = lax.rem(index, 2) == 0
    inner_perm, outer_perm = perms
    outer = lax.ppermute(jnp.where(even, low, high), axis, outer_perm)
    inner = lax.ppermute(jnp.where(even, high, low), axis, inner_perm)
    return jnp.where(even, outer, inner), jnp.where(even, inner, outer)


def all_sum(block):
    plane = lax.axis_size(PLANE)
    line = lax.axis_size(LINE)
    rows, cols = block.shape
    part = rows // plane
    mine = lax.all_to_all(block.reshape(plane, part, cols), PLANE, 0, 0, tiled=True).sum(0)
    mine = lax.all_to_all(
        jnp.broadcast_to(mine[None], (line, part, cols)), LINE, 0, 0, tiled=True
    ).sum(0)
    whole = lax.all_to_all(
        jnp.broadcast_to(mine[None], (plane, part, cols)), PLANE, 0, 0, tiled=True
    )
    return whole.reshape(rows, cols)


def shards(prior_ensemble, observed, obs_error, obs_index, obs_count):
    a = HALF_COURANT
    state = prior_ensemble.astype(jnp.float32)
    members, rows, cols = state.shape[1:]
    lat_index, lon_index = lax.axis_index(LAT), lax.axis_index(LON)
    lat_count, lon_count = lax.axis_size(LAT), lax.axis_size(LON)
    lat_perms = pair_perms(lat_count, False)
    lon_perms = pair_perms(lon_count, True)
    total_rows = rows * lat_count
    f = rotation_at(lat_index * rows - 1 + jnp.arange(4, dtype=jnp.int32), total_rows)
    has_south = (lat_index > 0).astype(jnp.float32)
    has_north = (lat_index < lat_count - 1).astype(jnp.float32)

    h, u, v = state[0], state[1], state[2]
    zero = jnp.zeros((members, 1), jnp.float32)

    def slope(row):
        row = jnp.concatenate([zero, row, zero], axis=1)
        return row[:, 2:] - row[:, :-2]

    down = jnp.stack([
        h[:, 0], v[:, 0],
        h[:, 0] - a * slope(u[:, 0]) - a * v[:, 1],
        v[:, 0] - a * h[:, 1] - f[1] * u[:, 0],
    ])
    up = jnp.stack([
        h[:, 1], v[:, 1],
        h[:, 1] - a * slope(u[:, 1]) + a * v[:, 0],
        v[:, 1] + a * h[:, 0] - f[2] * u[:, 1],
    ])
    south, north = swap(down, up, lat_index, LAT, lat_perms)

    edge = jnp.transpose(state, (0, 2, 3, 1))
    west, east = swap(edge[:, :, :2], edge[:, :, -2:], lon_index, LON, lon_perms)

    def corner(row):
        return jnp.stack([west[1, row, 1], east[1, row, 0], west[2, row, 1], east[2, row, 0]])

    south_corner, north_corner = swap(corner(0), corner(1), lat_index, LAT, lat_perms)

    west_t = jnp.transpose(west, (0, 3, 1, 2))
    east_t = jnp.transpose(east, (0, 3, 1, 2))
    wide = jnp.concatenate([west_t, state, east_t], axis=-1)
    wh, wu, wv = wide[0], wide[1], wide[2]

    def widen(row, corners):
        return jnp.concatenate([corners[2][:, None], row, corners[3][:, None]], axis=1)

    def mend(row, corners):
        return jnp.concatenate([
            (row[:, 0] + a * corners[0])[:, None], row[:, 1:-1],
            (row[:, -1] - a * corners[1])[:, None]], axis=1)

    south_v, north_v = widen(south[1], south_corner), widen(north[1], north_corner)
    v_above = jnp.stack([wv[:, 1, 1:-1], north_v], axis=1)
    v_below = jnp.stack([south_v, wv[:, 0, 1:-1]], axis=1)
    h_above = jnp.stack([h[:, 1], north[0]], axis=1)
    h_below = jnp.stack([south[0], h[:, 0]], axis=1)
    spin = f[1:3, None]
    rate_h = -a * ((wu[..., 2:] - wu[..., :-2]) + (v_above - v_below))
    rate_u = -a * (wh[..., 2:] - wh[..., :-2]) + spin * wv[..., 1:-1]
    rate_v = -a * (h_above - h_below) - spin * u
    mid_h = wh[..., 1:-1] + rate_h
    mid_u = wu[..., 1:-1] + rate_u
    mid_v = v + rate_v
    south_mid_h = has_south * (mend(south[2], south_corner) - a * v[:, 0])
    south_mid_v = has_south * (south[3] - a * h[:, 0])
    north_mid_h = has_north * (mend(north[2], north_corner) + a * v[:, 1])
    north_mid_v = has_north * (north[3] + a * h[:, 1])
    mid_v_above = jnp.stack([mid_v[:, 1], north_mid_v], axis=1)
    mid_v_below = jnp.stack([south_mid_v, mid_v[:, 0]], axis=1)
    mid_h_above = jnp.stack([mid_h[:, 1, 1:-1], north_mid_h], axis=1)
    mid_h_below = jnp.stack([south_mid_h, mid_h[:, 0, 1:-1]], axis=1)
    second_h = -a * ((mid_u[..., 2:] - mid_u[..., :-2]) + (mid_v_above - mid_v_below))
    second_u = -a * (mid_h[..., 2:] - mid_h[..., :-2]) + spin * mid_v
    second_v = -a * (mid_h_above - mid_h_below) - spin * mid_u[..., 1:-1]
    forecast = jnp.stack([
        h + 0.5 * (rate_h[..., 1:-1] + second_h),
        u + 0.5 * (rate_u[..., 1:-1] + second_u),
        v + 0.5 * (rate_v + second_v),
    ])

    center = jnp.mean(forecast, axis=1, keepdims=True)
    anomaly = forecast - center

    index = obs_index.reshape(-1)
    slots = index.shape[0]
    entries = 3 * rows * cols
    live = (jnp.arange(slots, dtype=jnp.int32) < obs_count.reshape(())).astype(jnp.float32)
    weight = live / obs_error.reshape(-1)
    weight = weight * weight
    named = (index[:, None] == jnp.arange(entries, dtype=jnp.int32)[None, :]).astype(jnp.float32)
    summed = jnp.dot(
        jnp.stack([weight, weight * observed.reshape(-1)]), named, precision=lax.Precision.HIGHEST
    ).reshape(2, 3, 1, rows, cols)
    weighted = anomaly * summed[0]
    pull = summed[1] - summed[0] * center
    gram = jnp.einsum("fmrc,fnrc->mn", weighted, anomaly, precision=lax.Precision.HIGHEST)
    push = jnp.einsum("frc,fnrc->n", pull[:, 0], anomaly, precision=lax.Precision.HIGHEST)

    row_at = jnp.arange(members)[:, None]
    col_at = jnp.arange(members)[None, :]
    sent = jnp.where((row_at == 0) & (col_at > 0), push[None, :], gram)
    sent = jnp.where((row_at == 1) & (col_at == 2), push[0], sent)
    total = all_sum(sent)
    push = jnp.where(jnp.arange(members) == 0, total[1, 2], total[0])
    lower = jnp.where(row_at >= col_at, total, 0.0)
    gram = lower + jnp.where(row_at > col_at, total, 0.0).T

    identity = jnp.eye(members, dtype=jnp.float32)
    prior = float(members - 1)
    factor = lax.linalg.cholesky(prior * identity + gram, symmetrize_input=False)
    inverse = lax.linalg.triangular_solve(factor, identity, left_side=True, lower=True)
    forward = jnp.dot(inverse, push, precision=lax.Precision.HIGHEST)
    mean_weights = jnp.dot(forward, inverse, precision=lax.Precision.HIGHEST)
    weights = math.sqrt(prior) * inverse + mean_weights[None, :]
    return center + jnp.einsum(
        "fmrc,jm->fjrc", anomaly, weights, precision=lax.Precision.HIGHEST
    )


def solution(mesh):
    lat, lon = mesh.shape["lat"], mesh.shape["lon"]
    parts = Mesh(mesh.devices.reshape(lat // 4, 2, 2, lon // 4, 4), LAT + LON)
    placed = (
        P(None, None, LAT, LON),
        P(LAT, LON, None),
        P(LAT, LON, None),
        P(LAT, LON, None),
        P(LAT, LON),
    )
    return jax.shard_map(
        shards, mesh=parts, in_specs=placed, out_specs=P(None, None, LAT, LON), check_vma=False
    )
```

time: 557 us -> 129 us (0.23)
  waiting for transfers between devices: 357 us -> 4.5 us
  blocking collectives: 119 us -> 50.3 us
  between operations: 14.3 us -> 1.05 us
    psum x1 -> x0, waiting for transfers between devices: 333 us -> none  [shards(): gram, push = lax.psum((local_gram, local_push), ('lat', 'lon'))]
    psum x1 -> x0, blocking collectives: 119 us -> none  [shards(): gram, push = lax.psum((local_gram, local_push), ('lat', 'lon'))]
    all_to_all x0 -> x3, blocking collectives: none -> 50.3 us  [the longest x1 20.9 us: all_sum(): lax.all_to_all(block.reshape(plane, part, cols), PLANE, 0, 0, tiled=True)]
    ppermute x4 -> x6, waiting for transfers between devices: 24.2 us -> 4.5 us  [the longest x3 4.49 us: swap(): outer = lax.ppermute(jnp.where(even, low, high), axis, outer_perm)]
    ppermute x4 -> x6, starting transfers between devices: 32.7 us -> 38.1 us  [the longest x3 32.3 us: swap(): outer = lax.ppermute(jnp.where(even, low, high), axis, outer_perm)]
    another operation x6 -> x9, other arithmetic: 12.9 us -> 12.8 us  [the longest x3 12.4 us: shards(): lax.linalg.cholesky(prior * identity + gram, symmetrize_input=False)]
  transfers between devices with their start and end apart: 5 -> 6, of which waited for: 4 -> 1; matrix products, arithmetic and copies ran while one was open for 0% -> 2% of each run, Pallas kernels for 0% -> 0%
where the time goes in v1:
time: 129 us; the launch traced here: 128 us
  blocking collectives  50.3 us (39%)
  starting transfers between devices  38.1 us (30%)
  other arithmetic  25.3 us (20%)
  local copies, waits for them, and re-layouts  5.17 us (4%)
  waiting for transfers between devices  4.5 us (3%)
  matrix products  3.92 us (3%)
    ppermute x3, starting transfers between devices, swap(): outer = lax.ppermute(jnp.where(even, low, high), axis, outer_perm)  32.3 us
    all_to_all x1, blocking collectives, all_sum(): lax.all_to_all(block.reshape(plane, part, cols), PLANE, 0, 0, tiled=True)  20.9 us
    all_to_all x1, blocking collectives, all_sum(): lax.all_to_all(jnp.broadcast_to(mine[None], (line, part, cols)), LINE, 0,...  17 us
    another operation x3, other arithmetic, shards(): lax.linalg.cholesky(prior * identity + gram, symmetrize_input=False)  12.4 us
    all_to_all x1, blocking collectives, all_sum(): lax.all_to_all(jnp.broadcast_to(mine[None], (plane, part, cols)), PLANE,...  12.3 us
    another operation x2, other arithmetic, shards(): lax.linalg.triangular_solve(factor, identity, left_side=True, lower=True)  10.5 us
    ppermute x3, starting transfers between devices, swap(): inner = lax.ppermute(jnp.where(even, high, low), axis, inner_perm)  5.76 us
    ppermute x3, waiting for transfers between devices, swap(): outer = lax.ppermute(jnp.where(even, low, high), axis, outer_perm)  4.49 us
  transfers between devices with their start and end apart: 6, of which 1 were waited for; matrix products, arithmetic and copies ran while one was open for 2% of the time, Pallas kernels for 0%

profile of v1, /device:TPU:1, one launch (start us, length us, event | category | flops | bytes accessed | tf_op | source)
XLA Modules:
  0.0 128.4 jit_solution(15061987265783510546)
XLA Ops:
  0.0 1.1 copy.27
  1.1 0.1 fusion.89
  1.2 16.2 %collective-permute-start = (f32[3,2,2,128]{3,2,1,0:T(2,128)S(1)}, f32[3,2,2,128]{3,2,1,0:T(2,128)S(1)}, u32[]{:S(2)}, u32[]{:S(2)}) collective-permute-start(f32[3,2,2,128]{3,2,1,0:T(2,128)S(1)} %get-tuple-element.25), channel_id=1, source_target_pairs={{1,2},{2,1},{3,4},{4,3},{5,6},{6,5},{7,8},{8,7},{9,10},{10,9},{11,... | collective-permute-start | bytes 18440 | tf_op jit(solution)/shard_map/ppermute | solution.py:35
  17.3 1.9 %collective-permute-start.1 = (f32[3,2,2,128]{3,2,1,0:T(2,128)S(1)}, f32[3,2,2,128]{3,2,1,0:T(2,128)S(1)}, u32[]{:S(2)}, u32[]{:S(2)}) collective-permute-start(f32[3,2,2,128]{3,2,1,0:T(2,128)S(1)} %get-tuple-element.26), channel_id=1, source_target_pairs={{0,1},{1,0},{2,3},{3,2},{4,5},{5,4},{6,7},{7,6},{8,9},{9,8},{10,11... | collective-permute-start | bytes 18440 | tf_op jit(solution)/shard_map/ppermute | solution.py:36
  19.3 0.7 fusion.94
  20.1 1.4 %bitcast_subtract_fusion.1 = (f32[1,128,128]{1,2,0:T(8,128)S(1)}, f32[1,128,128]{1,2,0:T(8,128)S(1)}) fusion(f32[128,2,128]{0,2,1:T(8,128)S(1)} %get-tuple-element.24, f32[]{:T(128)} %bitcast.24, f32[128,2,128]{0,2,1:T(8,128)S(1)} %get-tuple-element.23, f32[128,2,128]{0,2,1:T(8,128)S(1)} %get-tuple-element.22, f32[]{:T(128)} %bitcast.31), kind=kLoop, calls=%fused_computation.112 | loop fusion | flops 131072 | bytes 524296 | tf_op jit(solution)/shard_map/sub | solution.py:83
  21.5 0.0 copy-start.1
  21.5 8.8 %collective-permute-start.5 = (f32[4,128,128]{1,2,0:T(8,128)S(1)}, f32[4,128,128]{1,2,0:T(8,128)S(1)}, u32[]{:S(2)}, u32[]{:S(2)}) collective-permute-start(f32[4,128,128]{1,2,0:T(8,128)S(1)} %get-tuple-element.15), channel_id=1, source_target_pairs={{32,64},{64,32},{96,128},{128,96},{160,192},{192,160},{224,256},{2... | collective-permute-start | bytes 786440 | tf_op jit(solution)/shard_map/ppermute | solution.py:35
  30.3 1.9 %collective-permute-start.4 = (f32[4,128,128]{1,2,0:T(8,128)S(1)}, f32[4,128,128]{1,2,0:T(8,128)S(1)}, u32[]{:S(2)}, u32[]{:S(2)}) collective-permute-start(f32[4,128,128]{1,2,0:T(8,128)S(1)} %get-tuple-element.16), channel_id=1, source_target_pairs={{0,32},{32,0},{64,96},{96,64},{128,160},{160,128},{192,224},{224,1... | collective-permute-start | bytes 786440 | tf_op jit(solution)/shard_map/ppermute | solution.py:36
  32.9 0.0 copy-start
  32.9 0.0 copy-done.1
  32.9 0.7 copy-done
  33.6 0.0 copy-start.2
  33.6 0.7 copy-done.2
  34.3 0.4 fusion.3
  34.7 0.1 slice.301
  34.8 0.0 collective-permute-done
  34.8 0.0 collective-permute-done.1
  34.9 7.4 %collective-permute-start.3 = (f32[4,128]{1,0:T(4,128)S(1)}, f32[4,128]{1,0:T(4,128)S(1)}, u32[]{:S(2)}, u32[]{:S(2)}) collective-permute-start(f32[4,128]{1,0:T(4,128)S(1)} %get-tuple-element.75), channel_id=1, source_target_pairs={{32,64},{64,32},{96,128},{128,96},{160,192},{192,160},{224,256},{2... | collective-permute-start | bytes 6152 | tf_op jit(solution)/shard_map/ppermute | solution.py:35
  42.2 1.9 %collective-permute-start.2 = (f32[4,128]{1,0:T(4,128)S(1)}, f32[4,128]{1,0:T(4,128)S(1)}, u32[]{:S(2)}, u32[]{:S(2)}) collective-permute-start(f32[4,128]{1,0:T(4,128)S(1)} %get-tuple-element.76), channel_id=1, source_target_pairs={{0,32},{32,0},{64,96},{96,64},{128,160},{160,128},{192,224},{224,1... | collective-permute-start | bytes 6152 | tf_op jit(solution)/shard_map/ppermute | solution.py:36
  44.3 4.5 %collective-permute-done.3 = f32[4,128]{1,0:T(4,128)S(1)} collective-permute-done((f32[4,128]{1,0:T(4,128)S(1)}, f32[4,128]{1,0:T(4,128)S(1)}, u32[]{:S(2)}, u32[]{:S(2)}) %collective-permute-start.3) | collective-permute-done | bytes 2080 | tf_op jit(solution)/shard_map/ppermute | solution.py:35
  48.8 0.0 collective-permute-done.2
  48.8 0.0 collective-permute-done.5
  48.8 0.0 collective-permute-done.4
  49.0 0.1 slice_add_fusion
  49.2 0.1 fusion.29
  49.3 0.1 fusion.23
  49.5 0.1 fusion.35
  49.5 0.2 fusion.62
  49.7 0.4 convolution_bitcast_fusion.1
  50.1 1.2 fusion.2
  51.4 20.9 %all_to_all.15 = f32[32,4,128]{2,1,0:T(4,128)S(1)} all-to-all(f32[32,4,128]{2,1,0:T(4,128)S(1)} %bitcast.215), channel_id=1, replica_groups=mesh['x'=4,'zh'=2,'core'=2,'zl'=8,'y'=4] {'x','core','y'}, dimensions={0} | all-to-all | bytes 131072 | tf_op jit(solution)/shard_map/all_to_all | solution.py:45
  72.4 17.0 %all_to_all.16 = f32[16,4,128]{2,1,0:T(4,128)S(1)} all-to-all(f32[16,4,128]{2,1,0:T(4,128)S(1)} %broadcast_in_dim.23), channel_id=1, replica_groups=mesh['x'=4,'zh'=2,'core'=2,'zl'=8,'y'=4] {'zh','zl'}, dimensions={0} | all-to-all | bytes 65536 | tf_op jit(solution)/shard_map/all_to_all | solution.py:46
  89.4 12.3 %all_to_all.17 = f32[32,4,128]{2,1,0:T(4,128)S(1)} all-to-all(f32[32,4,128]{2,1,0:T(4,128)S(1)} %broadcast_in_dim.24), channel_id=1, replica_groups=mesh['x'=4,'zh'=2,'core'=2,'zl'=8,'y'=4] {'x','core','y'}, dimensions={0} | all-to-all | bytes 131072 | tf_op jit(solution)/shard_map/all_to_all | solution.py:49
  101.8 0.6 slice.393
  102.4 0.1 copy.31
  102.5 11.7 %cholesky.17 = f32[128,128]{1,0:T(8,128)S(1)} custom-call(f32[128,128]{1,0:T(8,128)S(1)} %fusion.59), custom_call_target="Cholesky" | custom-call | tf_op jit(solution)/shard_map/cholesky | solution.py:166
  114.3 0.6 compare_reduce_fusion
  114.9 0.7 fusion.49
  115.6 9.8 %custom-call.5 = f32[1,128,128]{1,2,0:T(8,128)S(1)} custom-call(f32[1,128,128]{2,1,0:T(8,128)S(1)} %fusion.49), custom_call_target="InvertDiagBlocksLowerTriangular" | custom-call | tf_op jit(solution)/shard_map/triangular_solve | solution.py:167
  125.4 0.2 fusion.57
  125.7 0.8 convolution_bitcast_fusion.3
  126.5 0.2 convolution_bitcast_fusion.2
  126.7 0.6 fusion
  127.3 1.1 copy.34
  (40 shorter events, 0.7 us)
Async XLA Ops:
  1.2 33.6 %collective-permute-start = (f32[3,2,2,128]{3,2,1,0:T(2,128)S(1)}, f32[3,2,2,128]{3,2,1,0:T(2,128)S(1)}, u32[]{:S(2)}, u32[]{:S(2)}) collective-permute-start(f32[3,2,2,128]{3,2,1,0:T(2,128)S(1)} %get-tuple-element.25), channel_id=1, source_target_pairs={{1,2},{2,1},{3,4},{4,3},{5,6},{6,5},{7,8},{8,7},{9,10},{10,9},{11,... | collective-permute-start | bytes 18440 | tf_op jit(solution)/shard_map/ppermute | solution.py:35
  17.3 17.5 %collective-permute-start.1 = (f32[3,2,2,128]{3,2,1,0:T(2,128)S(1)}, f32[3,2,2,128]{3,2,1,0:T(2,128)S(1)}, u32[]{:S(2)}, u32[]{:S(2)}) collective-permute-start(f32[3,2,2,128]{3,2,1,0:T(2,128)S(1)} %get-tuple-element.26), channel_id=1, source_target_pairs={{0,1},{1,0},{2,3},{3,2},{4,5},{5,4},{6,7},{7,6},{8,9},{9,8},{10,11... | collective-permute-start | bytes 18440 | tf_op jit(solution)/shard_map/ppermute | solution.py:36
  21.5 11.5 %copy-start.1 = (f32[1,1,256]{2,1,0:T(1,128)S(1)}, f32[1,1,256]{2,1,0:T(1,128)}, u32[]{:S(2)}) copy-start(f32[1,1,256]{2,1,0:T(1,128)} %param.7) | copy-start | bytes 3076
  21.5 27.2 %collective-permute-start.5 = (f32[4,128,128]{1,2,0:T(8,128)S(1)}, f32[4,128,128]{1,2,0:T(8,128)S(1)}, u32[]{:S(2)}, u32[]{:S(2)}) collective-permute-start(f32[4,128,128]{1,2,0:T(8,128)S(1)} %get-tuple-element.15), channel_id=1, source_target_pairs={{32,64},{64,32},{96,128},{128,96},{160,192},{192,160},{224,256},{2... | collective-permute-start | bytes 786440 | tf_op jit(solution)/shard_map/ppermute | solution.py:35
  30.3 18.5 %collective-permute-start.4 = (f32[4,128,128]{1,2,0:T(8,128)S(1)}, f32[4,128,128]{1,2,0:T(8,128)S(1)}, u32[]{:S(2)}, u32[]{:S(2)}) collective-permute-start(f32[4,128,128]{1,2,0:T(8,128)S(1)} %get-tuple-element.16), channel_id=1, source_target_pairs={{0,32},{32,0},{64,96},{96,64},{128,160},{160,128},{192,224},{224,1... | collective-permute-start | bytes 786440 | tf_op jit(solution)/shard_map/ppermute | solution.py:36
  32.9 0.7 copy-start
  33.6 0.7 copy-start.2
  34.9 13.9 %collective-permute-start.3 = (f32[4,128]{1,0:T(4,128)S(1)}, f32[4,128]{1,0:T(4,128)S(1)}, u32[]{:S(2)}, u32[]{:S(2)}) collective-permute-start(f32[4,128]{1,0:T(4,128)S(1)} %get-tuple-element.75), channel_id=1, source_target_pairs={{32,64},{64,32},{96,128},{128,96},{160,192},{192,160},{224,256},{2... | collective-permute-start | bytes 6152 | tf_op jit(solution)/shard_map/ppermute | solution.py:35
  42.2 6.5 %collective-permute-start.2 = (f32[4,128]{1,0:T(4,128)S(1)}, f32[4,128]{1,0:T(4,128)S(1)}, u32[]{:S(2)}, u32[]{:S(2)}) collective-permute-start(f32[4,128]{1,0:T(4,128)S(1)} %get-tuple-element.76), channel_id=1, source_target_pairs={{0,32},{32,0},{64,96},{96,64},{128,160},{160,128},{192,224},{224,1... | collective-permute-start | bytes 6152 | tf_op jit(solution)/shard_map/ppermute | solution.py:36

commit v2 on v1

--- a/solution.py
+++ b/solution.py
@@ -3,6 +3,8 @@
 import jax
 import jax.numpy as jnp
 from jax import lax
+from jax.experimental import pallas as pl
+from jax.experimental.pallas import tpu as pltpu
 from jax.sharding import Mesh, PartitionSpec as P
 
 HALF_COURANT = 0.4
@@ -12,6 +14,8 @@
 LON = ("zl", "y")
 PLANE = ("x", "core", "y")
 LINE = ("zh", "zl")
+MEMBERS = 128
+PANEL = 8
 
 
 def rotation_at(rows, total_rows):
@@ -52,6 +56,88 @@
     return whole.reshape(rows, cols)
 
 
+def splat(tile, lane):
+    return jnp.broadcast_to(tile[:, lane:lane + 1], tile.shape)
+
+def thirds(x):
+    hi = x.astype(jnp.bfloat16).astype(jnp.float32)
+    rest = x - hi
+    mid = rest.astype(jnp.bfloat16).astype(jnp.float32)
+    return hi, mid, rest - mid
+
+def outer_sum(left, whole):
+    a, b, c = thirds(left)
+    d, e, f = thirds(whole)
+    first = jnp.concatenate([a, a, b, a, c, b], axis=0).astype(jnp.bfloat16)
+    second = jnp.concatenate([d, e, d, f, d, e], axis=0).astype(jnp.bfloat16)
+    return lax.dot_general(first, second, (((0,), (0,)), ((), ())), preferred_element_type=jnp.float32)
+
+def eliminate(aug):
+    sub = lax.broadcasted_iota(jnp.int32, (PANEL, MEMBERS), 0)
+    def fetch(i):
+        return (jnp.broadcast_to(aug[i:i+1, :MEMBERS], (PANEL, MEMBERS)), jnp.broadcast_to(aug[i:i+1, MEMBERS:], (PANEL, MEMBERS)))
+    left, right = zip(*[fetch(i) for i in range(PANEL)])
+    left, right = list(left), list(right)
+    s = {(i, k): splat(left[i], k) for i in range(PANEL) for k in range(i, PANEL)}
+    for p in range(MEMBERS // PANEL):
+        for j in range(PANEL):
+            r = lax.rsqrt(s[j, j])
+            left[j] = left[j] * r
+            right[j] = right[j] * r
+            l = {i: s[j, i] * r for i in range(j + 1, PANEL)}
+            for i in range(j + 1, PANEL):
+                for k in range(i, PANEL):
+                    s[i, k] = s[i, k] - l[i] * l[k]
+                left[i] = left[i] - l[i] * left[j]
+                right[i] = right[i] - l[i] * right[j]
+        tl, tr = left[0], right[0]
+        for j in range(1, PANEL):
+            tl = jnp.where(sub == j, left[j], tl)
+            tr = jnp.where(sub == j, right[j], tr)
+        aug[p*PANEL:(p+1)*PANEL, MEMBERS:] = tr
+        q = p + 1
+        if q * PANEL < MEMBERS:
+            base = q * PANEL
+            t = {(j, i): splat(left[j], base + i) for j in range(PANEL) for i in range(PANEL)}
+            nl, nr, ns = [], [], {}
+            for i in range(PANEL):
+                a, b = fetch(base + i)
+                for k in range(i, PANEL):
+                    acc = splat(a, base + k)
+                    for j in range(PANEL):
+                        acc = acc - t[j, i] * t[j, k]
+                    ns[i, k] = acc
+                for j in range(PANEL):
+                    a = a - t[j, i] * left[j]
+                    b = b - t[j, i] * right[j]
+                nl.append(a); nr.append(b)
+            if base + PANEL < MEMBERS:
+                prod = outer_sum(tl, jnp.concatenate([tl, tr], axis=1))
+                aug[base + PANEL:, :] = aug[base + PANEL:, :] - prod[base + PANEL:, :]
+            left, right, s = nl, nr, ns
+
+def finish(total_ref, x_ref, c_ref, o_ref, aug):
+    total = total_ref[...]
+    row = lax.broadcasted_iota(jnp.int32, (MEMBERS, MEMBERS), 0)
+    col = lax.broadcasted_iota(jnp.int32, (MEMBERS, MEMBERS), 1)
+    prior = float(MEMBERS - 1)
+    unit = jnp.where(row == col, 1.0, 0.0)
+    aug[:, :MEMBERS] = jnp.where(col >= row, total, 0.0) + prior * unit
+    aug[:, MEMBERS:] = unit
+    eliminate(aug)
+    inverse = aug[:, MEMBERS:]
+    lane = lax.broadcasted_iota(jnp.int32, (8, MEMBERS), 1)
+    push = jnp.where(lane == MEMBERS - 1, jnp.broadcast_to(total[MEMBERS-2:MEMBERS-1, 0:1], (8, MEMBERS)), jnp.broadcast_to(total[MEMBERS-1:MEMBERS, :], (8, MEMBERS)))
+    forward = lax.dot_general(push, inverse, (((1,), (1,)), ((), ())), precision=lax.Precision.HIGHEST, preferred_element_type=jnp.float32)
+    mean_weights = jnp.dot(forward, inverse, precision=lax.Precision.HIGHEST, preferred_element_type=jnp.float32)
+    weights = math.sqrt(prior) * inverse + mean_weights[0:1, :]
+    for f in range(3):
+        for r in range(2):
+            k = 2 * f + r
+            post = lax.dot_general(weights, x_ref[k * MEMBERS:(k + 1) * MEMBERS, :], (((1,), (1,)), ((), ())), precision=lax.Precision.HIGHEST, preferred_element_type=jnp.float32)
+            o_ref[pl.ds(f * 2 * MEMBERS + r, MEMBERS, stride=2), :] = post + c_ref[k:k+1, :]
+
+
 def shards(prior_ensemble, observed, obs_error, obs_index, obs_count):
     a = HALF_COURANT
     state = prior_ensemble.astype(jnp.float32)
@@ -82,9 +168,10 @@
         h[:, 1] - a * slope(u[:, 1]) + a * v[:, 0],
         v[:, 1] + a * h[:, 0] - f[2] * u[:, 1],
     ])
+    down, up, edge = lax.optimization_barrier((down, up, state))
     south, north = swap(down, up, lat_index, LAT, lat_perms)
 
-    edge = jnp.transpose(state, (0, 2, 3, 1))
+    edge = jnp.transpose(edge, (0, 2, 3, 1))
     west, east = swap(edge[:, :, :2], edge[:, :, -2:], lon_index, LON, lon_perms)
 
     def corner(row):
@@ -154,23 +241,18 @@
 
     row_at = jnp.arange(members)[:, None]
     col_at = jnp.arange(members)[None, :]
-    sent = jnp.where((row_at == 0) & (col_at > 0), push[None, :], gram)
-    sent = jnp.where((row_at == 1) & (col_at == 2), push[0], sent)
+    sent = jnp.where((row_at == members - 1) & (col_at < members - 1), push[None, :], gram)
+    sent = jnp.where((row_at == members - 2) & (col_at == 0), push[members - 1], sent)
     total = all_sum(sent)
-    push = jnp.where(jnp.arange(members) == 0, total[1, 2], total[0])
-    lower = jnp.where(row_at >= col_at, total, 0.0)
-    gram = lower + jnp.where(row_at > col_at, total, 0.0).T
-
-    identity = jnp.eye(members, dtype=jnp.float32)
-    prior = float(members - 1)
-    factor = lax.linalg.cholesky(prior * identity + gram, symmetrize_input=False)
-    inverse = lax.linalg.triangular_solve(factor, identity, left_side=True, lower=True)
-    forward = jnp.dot(inverse, push, precision=lax.Precision.HIGHEST)
-    mean_weights = jnp.dot(forward, inverse, precision=lax.Precision.HIGHEST)
-    weights = math.sqrt(prior) * inverse + mean_weights[None, :]
-    return center + jnp.einsum(
-        "fmrc,jm->fjrc", anomaly, weights, precision=lax.Precision.HIGHEST
-    )
+    entries_first = jnp.transpose(anomaly, (0, 2, 3, 1)).reshape(entries, members)
+    posterior = pl.pallas_call(
+        finish,
+        out_shape=jax.ShapeDtypeStruct((3 * rows * members, cols), jnp.float32),
+        scratch_shapes=[pltpu.VMEM((members, 2 * members), jnp.float32)],
+        compiler_params=pltpu.CompilerParams(vmem_limit_bytes=16 * 1024 * 1024),
+        cost_estimate=pl.CostEstimate(flops=3 * 10**7, bytes_accessed=10**6, transcendentals=0),
+    )(total, entries_first, center.reshape(3 * rows, cols))
+    return posterior.reshape(3, members, rows, cols)
 
 
 def solution(mesh):

time: 129 us -> 120 us (0.930)
  other arithmetic: 25.3 us -> 2.57 us
  waiting for transfers between devices: 4.5 us -> 24.5 us
  blocking collectives: 50.3 us -> 36.5 us
  Pallas kernels: 0 us -> 5.9 us
  starting transfers between devices: 38.1 us -> 41.9 us
  matrix products: 3.92 us -> 2.26 us
    another operation x5 -> x1, other arithmetic: 22.9 us -> 0.02 us  [shards(): jnp.stack([h[:, 0], v[:, 0], h[:, 0] - a * slope(u[:, 0]) - a * v[:, 1],...]
    ppermute x3, waiting for transfers between devices: 4.49 us -> 17.1 us  [swap(): outer = lax.ppermute(jnp.where(even, low, high), axis, outer_perm)]
    all_to_all x1 -> x0, blocking collectives: 12.3 us -> none  [all_sum(): lax.all_to_all(jnp.broadcast_to(mine[None], (plane, part, cols)), PLANE,...]
    ppermute x3, starting transfers between devices: 32.3 us -> 24 us  [swap(): outer = lax.ppermute(jnp.where(even, low, high), axis, outer_perm)]
    all_to_all x0 -> x1, waiting for transfers between devices: none -> 7.34 us  [all_sum(): lax.all_to_all(jnp.broadcast_to(mine[None], (plane, part, cols)), PLANE,...]
    ppermute x3, starting transfers between devices: 5.76 us -> 12.6 us  [swap(): inner = lax.ppermute(jnp.where(even, high, low), axis, inner_perm)]
    pallas_call x0 -> x1, Pallas kernels: none -> 5.9 us  [shards(): pl.pallas_call(finish, out_shape=jax.ShapeDtypeStruct((3 * rows * members...]
    all_to_all x0 -> x1, starting transfers between devices: none -> 5.28 us  [all_sum(): lax.all_to_all(jnp.broadcast_to(mine[None], (plane, part, cols)), PLANE,...]
  transfers between devices with their start and end apart: 6 -> 7, of which waited for: 1 -> 3; matrix products, arithmetic and copies ran while one was open for 2% -> 1% of each run, Pallas kernels for 0% -> 0%
where the time goes in v2:
time: 120 us; the launch traced here: 119 us
  starting transfers between devices  41.9 us (35%)
  blocking collectives  36.5 us (30%)
  waiting for transfers between devices  24.5 us (20%)
  Pallas kernels  5.9 us (5%)
  local copies, waits for them, and re-layouts  4.6 us (4%)
  other arithmetic  2.57 us (2%)
  matrix products  2.26 us (2%)
    ppermute x3, starting transfers between devices, swap(): outer = lax.ppermute(jnp.where(even, low, high), axis, outer_perm)  24 us
    all_to_all x1, blocking collectives, all_sum(): lax.all_to_all(jnp.broadcast_to(mine[None], (line, part, cols)), LINE, 0,...  18.8 us
    all_to_all x1, blocking collectives, all_sum(): lax.all_to_all(block.reshape(plane, part, cols), PLANE, 0, 0, tiled=True)  17.7 us
    ppermute x3, waiting for transfers between devices, swap(): outer = lax.ppermute(jnp.where(even, low, high), axis, outer_perm)  17.1 us
    ppermute x3, starting transfers between devices, swap(): inner = lax.ppermute(jnp.where(even, high, low), axis, inner_perm)  12.6 us
    all_to_all x1, waiting for transfers between devices, all_sum(): lax.all_to_all(jnp.broadcast_to(mine[None], (plane, part, cols)), PLANE,...  7.34 us
    pallas_call x1, Pallas kernels, shards(): pl.pallas_call(finish, out_shape=jax.ShapeDtypeStruct((3 * rows * members...  5.9 us
    all_to_all x1, starting transfers between devices, all_sum(): lax.all_to_all(jnp.broadcast_to(mine[None], (plane, part, cols)), PLANE,...  5.28 us
  transfers between devices with their start and end apart: 7, of which 3 were waited for; matrix products, arithmetic and copies ran while one was open for 1% of the time, Pallas kernels for 0%

profile of v2, /device:TPU:1, one launch (start us, length us, event | category | flops | bytes accessed | tf_op | source)
XLA Modules:
  0.0 119.2 jit_solution(771352213140175612)
XLA Ops:
  0.0 0.6 fusion.67
  0.7 1.1 copy.12
  1.9 1.3 %bitcast_subtract_fusion = (f32[1,128,128]{1,2,0:T(8,128)S(1)}, f32[1,128,128]{1,2,0:T(8,128)S(1)}) fusion(f32[128,2,128]{0,2,1:T(8,128)S(1)} %get-tuple-element.31, f32[]{:T(128)} %bitcast.23, f32[128,2,128]{0,2,1:T(8,128)S(1)} %get-tuple-element.32, f32[128,2,128]{0,2,1:T(8,128)S(1)} %get-tuple-element.30, f32[]{:T(128)} %bitcast.16), kind=kLoop, calls=%fused_computation.95 | loop fusion | flops 131072 | bytes 524296 | tf_op jit(solution)/shard_map/sub | solution.py:169
  3.3 8.8 %collective-permute-start.4 = (f32[4,128,128]{1,2,0:T(8,128)S(1)}, f32[4,128,128]{1,2,0:T(8,128)S(1)}, u32[]{:S(2)}, u32[]{:S(2)}) collective-permute-start(f32[4,128,128]{1,2,0:T(8,128)S(1)} %get-tuple-element.22), channel_id=1, source_target_pairs={{0,32},{32,0},{64,96},{96,64},{128,160},{160,128},{192,224},{224,1... | collective-permute-start | bytes 786440 | tf_op jit(solution)/shard_map/ppermute | solution.py:40
  12.1 10.0 %collective-permute-start.5 = (f32[4,128,128]{1,2,0:T(8,128)S(1)}, f32[4,128,128]{1,2,0:T(8,128)S(1)}, u32[]{:S(2)}, u32[]{:S(2)}) collective-permute-start(f32[4,128,128]{1,2,0:T(8,128)S(1)} %get-tuple-element.21), channel_id=1, source_target_pairs={{32,64},{64,32},{96,128},{128,96},{160,192},{192,160},{224,256},{2... | collective-permute-start | bytes 786440 | tf_op jit(solution)/shard_map/ppermute | solution.py:39
  22.1 0.0 copy-start.1
  22.2 7.8 %collective-permute-start = (f32[3,2,2,128]{3,2,1,0:T(2,128)S(1)}, f32[3,2,2,128]{3,2,1,0:T(2,128)S(1)}, u32[]{:S(2)}, u32[]{:S(2)}) collective-permute-start(f32[3,2,2,128]{3,2,1,0:T(2,128)S(1)} %get-tuple-element.26), channel_id=1, source_target_pairs={{1,2},{2,1},{3,4},{4,3},{5,6},{6,5},{7,8},{8,7},{9,10},{10,9},{11,... | collective-permute-start | bytes 18440 | tf_op jit(solution)/shard_map/ppermute | solution.py:39
  30.0 1.9 %collective-permute-start.1 = (f32[3,2,2,128]{3,2,1,0:T(2,128)S(1)}, f32[3,2,2,128]{3,2,1,0:T(2,128)S(1)}, u32[]{:S(2)}, u32[]{:S(2)}) collective-permute-start(f32[3,2,2,128]{3,2,1,0:T(2,128)S(1)} %get-tuple-element.27), channel_id=1, source_target_pairs={{0,1},{1,0},{2,3},{3,2},{4,5},{5,4},{6,7},{7,6},{8,9},{9,8},{10,11... | collective-permute-start | bytes 18440 | tf_op jit(solution)/shard_map/ppermute | solution.py:40
  32.6 0.0 copy-start
  32.6 0.0 copy-done.1
  32.6 0.7 copy-done
  33.3 0.0 copy-start.2
  33.3 0.7 copy-done.2
  34.0 0.4 fusion.2
  34.4 0.1 slice.289
  34.5 9.8 %collective-permute-done = f32[3,2,2,128]{3,2,1,0:T(2,128)S(1)} collective-permute-done((f32[3,2,2,128]{3,2,1,0:T(2,128)S(1)}, f32[3,2,2,128]{3,2,1,0:T(2,128)S(1)}, u32[]{:S(2)}, u32[]{:S(2)}) %collective-permute-start) | collective-permute-done | bytes 6176 | tf_op jit(solution)/shard_map/ppermute | solution.py:39
  44.3 0.0 collective-permute-done.1
  44.4 1.9 %collective-permute-start.2 = (f32[4,128]{1,0:T(4,128)S(1)}, f32[4,128]{1,0:T(4,128)S(1)}, u32[]{:S(2)}, u32[]{:S(2)}) collective-permute-start(f32[4,128]{1,0:T(4,128)S(1)} %get-tuple-element.80), channel_id=1, source_target_pairs={{0,32},{32,0},{64,96},{96,64},{128,160},{160,128},{192,224},{224,1... | collective-permute-start | bytes 6152 | tf_op jit(solution)/shard_map/ppermute | solution.py:40
  46.3 6.2 %collective-permute-start.3 = (f32[4,128]{1,0:T(4,128)S(1)}, f32[4,128]{1,0:T(4,128)S(1)}, u32[]{:S(2)}, u32[]{:S(2)}) collective-permute-start(f32[4,128]{1,0:T(4,128)S(1)} %get-tuple-element.79), channel_id=1, source_target_pairs={{32,64},{64,32},{96,128},{128,96},{160,192},{192,160},{224,256},{2... | collective-permute-start | bytes 6152 | tf_op jit(solution)/shard_map/ppermute | solution.py:39
  52.6 0.0 collective-permute-done.2
  52.6 7.3 %collective-permute-done.3 = f32[4,128]{1,0:T(4,128)S(1)} collective-permute-done((f32[4,128]{1,0:T(4,128)S(1)}, f32[4,128]{1,0:T(4,128)S(1)}, u32[]{:S(2)}, u32[]{:S(2)}) %collective-permute-start.3) | collective-permute-done | bytes 2080 | tf_op jit(solution)/shard_map/ppermute | solution.py:39
  59.9 0.0 collective-permute-done.4
  59.9 0.0 collective-permute-done.5
  60.1 0.1 slice_add_fusion
  60.3 0.1 fusion.43
  60.3 0.1 fusion.22
  60.5 0.1 fusion.16
  60.6 0.1 fusion.28
  60.7 0.2 fusion.6
  60.9 0.2 fusion.5
  61.0 0.3 convolution_bitcast_fusion.1
  61.3 0.6 slice.318
  61.9 1.6 %fusion.1 = f32[128,128]{1,0:T(8,128)S(1)} fusion(f32[3,128,2,128]{1,3,2,0:T(8,128)S(1)} %fusion.5, f32[3,2,128]{2,1,0:T(2,128)S(1)} %bitcast.187, f32[128]{0:T(128)S(1)} %convolution_bitcast_fusion.1, f32[]{:T(128)} %bitcast.70, pred[128]{0:T(512)(128)(4,1)S(1)} %get-tuple-element.93, pred[128]{0:T(512)(128)(4,1)S(1)} %get-tuple-element.95, ...), kind=kOutput, calls=%fused_computation.2 | convolution fusion | flops 151158784 | bytes 462852 | tf_op jit(solution)/shard_map/fmrc,fnrc->mn/dot_general | solution.py:239
  63.5 17.7 %all_to_all.15 = f32[32,4,128]{2,1,0:T(4,128)S(1)} all-to-all(f32[32,4,128]{2,1,0:T(4,128)S(1)} %bitcast.183), channel_id=1, replica_groups=mesh['x'=4,'zh'=2,'core'=2,'zl'=8,'y'=4] {'x','core','y'}, dimensions={0} | all-to-all | bytes 131072 | tf_op jit(solution)/shard_map/all_to_all | solution.py:49
  81.3 18.8 %all_to_all.16 = f32[16,4,128]{2,1,0:T(4,128)S(1)} all-to-all(f32[16,4,128]{2,1,0:T(4,128)S(1)} %broadcast_in_dim.18), channel_id=1, replica_groups=mesh['x'=4,'zh'=2,'core'=2,'zl'=8,'y'=4] {'zh','zl'}, dimensions={0} | all-to-all | bytes 65536 | tf_op jit(solution)/shard_map/all_to_all | solution.py:50
  100.0 0.6 broadcast_in_dim.19
  100.7 5.3 %all-to-all-start.2 = ((f32[32,4,128]{2,1,0:T(4,128)}), f32[32,4,128]{2,1,0:T(4,128)S(1)}, u32[]{:S(2)}, u32[]{:S(2)}) async-start(f32[32,4,128]{2,1,0:T(4,128)} %broadcast_in_dim.19), calls=%async_computation.2 | async-start | bytes 131072 | tf_op jit(solution)/shard_map/all_to_all | solution.py:53
  106.0 7.3 %all-to-all-done.2 = f32[32,4,128]{2,1,0:T(4,128)S(1)} async-done(((f32[32,4,128]{2,1,0:T(4,128)}), f32[32,4,128]{2,1,0:T(4,128)S(1)}, u32[]{:S(2)}, u32[]{:S(2)}) %all-to-all-start.2) | async-done | bytes 65568 | tf_op jit(solution)/shard_map/all_to_all | solution.py:53
  113.3 5.9 %shard_map.55 = f32[768,128]{1,0:T(8,128)} custom-call(f32[128,128]{1,0:T(8,128)S(1)} %bitcast.181, f32[768,128]{1,0:T(8,128)S(1)} %bitcast.180, f32[6,128]{1,0:T(8,128)S(1)} %div.32.c_ref), custom_call_target="tpu_custom_call" | custom-call | flops 30000000 | bytes 1000000 | tf_op jit(solution)/shard_map/pallas_call | solution.py:248
  (40 shorter events, 0.7 us)
Async XLA Ops:
  3.3 56.6 %collective-permute-start.4 = (f32[4,128,128]{1,2,0:T(8,128)S(1)}, f32[4,128,128]{1,2,0:T(8,128)S(1)}, u32[]{:S(2)}, u32[]{:S(2)}) collective-permute-start(f32[4,128,128]{1,2,0:T(8,128)S(1)} %get-tuple-element.22), channel_id=1, source_target_pairs={{0,32},{32,0},{64,96},{96,64},{128,160},{160,128},{192,224},{224,1... | collective-permute-start | bytes 786440 | tf_op jit(solution)/shard_map/ppermute | solution.py:40
  12.1 47.8 %collective-permute-start.5 = (f32[4,128,128]{1,2,0:T(8,128)S(1)}, f32[4,128,128]{1,2,0:T(8,128)S(1)}, u32[]{:S(2)}, u32[]{:S(2)}) collective-permute-start(f32[4,128,128]{1,2,0:T(8,128)S(1)} %get-tuple-element.21), channel_id=1, source_target_pairs={{32,64},{64,32},{96,128},{128,96},{160,192},{192,160},{224,256},{2... | collective-permute-start | bytes 786440 | tf_op jit(solution)/shard_map/ppermute | solution.py:39
  22.1 10.5 %copy-start.1 = (f32[1,1,256]{2,1,0:T(1,128)S(1)}, f32[1,1,256]{2,1,0:T(1,128)}, u32[]{:S(2)}) copy-start(f32[1,1,256]{2,1,0:T(1,128)} %param.7) | copy-start | bytes 3076
  22.2 22.1 %collective-permute-start = (f32[3,2,2,128]{3,2,1,0:T(2,128)S(1)}, f32[3,2,2,128]{3,2,1,0:T(2,128)S(1)}, u32[]{:S(2)}, u32[]{:S(2)}) collective-permute-start(f32[3,2,2,128]{3,2,1,0:T(2,128)S(1)} %get-tuple-element.26), channel_id=1, source_target_pairs={{1,2},{2,1},{3,4},{4,3},{5,6},{6,5},{7,8},{8,7},{9,10},{10,9},{11,... | collective-permute-start | bytes 18440 | tf_op jit(solution)/shard_map/ppermute | solution.py:39
  30.0 14.3 %collective-permute-start.1 = (f32[3,2,2,128]{3,2,1,0:T(2,128)S(1)}, f32[3,2,2,128]{3,2,1,0:T(2,128)S(1)}, u32[]{:S(2)}, u32[]{:S(2)}) collective-permute-start(f32[3,2,2,128]{3,2,1,0:T(2,128)S(1)} %get-tuple-element.27), channel_id=1, source_target_pairs={{0,1},{1,0},{2,3},{3,2},{4,5},{5,4},{6,7},{7,6},{8,9},{9,8},{10,11... | collective-permute-start | bytes 18440 | tf_op jit(solution)/shard_map/ppermute | solution.py:40
  32.6 0.7 copy-start
  33.3 0.7 copy-start.2
  44.4 8.2 %collective-permute-start.2 = (f32[4,128]{1,0:T(4,128)S(1)}, f32[4,128]{1,0:T(4,128)S(1)}, u32[]{:S(2)}, u32[]{:S(2)}) collective-permute-start(f32[4,128]{1,0:T(4,128)S(1)} %get-tuple-element.80), channel_id=1, source_target_pairs={{0,32},{32,0},{64,96},{96,64},{128,160},{160,128},{192,224},{224,1... | collective-permute-start | bytes 6152 | tf_op jit(solution)/shard_map/ppermute | solution.py:40
  46.3 13.6 %collective-permute-start.3 = (f32[4,128]{1,0:T(4,128)S(1)}, f32[4,128]{1,0:T(4,128)S(1)}, u32[]{:S(2)}, u32[]{:S(2)}) collective-permute-start(f32[4,128]{1,0:T(4,128)S(1)} %get-tuple-element.79), channel_id=1, source_target_pairs={{32,64},{64,32},{96,128},{128,96},{160,192},{192,160},{224,256},{2... | collective-permute-start | bytes 6152 | tf_op jit(solution)/shard_map/ppermute | solution.py:39
  100.7 12.6 %all-to-all-start.2 = ((f32[32,4,128]{2,1,0:T(4,128)}), f32[32,4,128]{2,1,0:T(4,128)S(1)}, u32[]{:S(2)}, u32[]{:S(2)}) async-start(f32[32,4,128]{2,1,0:T(4,128)} %broadcast_in_dim.19), calls=%async_computation.2 | async-start | bytes 131072 | tf_op jit(solution)/shard_map/all_to_all | solution.py:53

commit v3 on v2

--- a/solution.py
+++ b/solution.py
@@ -33,8 +33,7 @@
     return inner, outer
 
 
-def swap(low, high, index, axis, perms):
-    even = lax.rem(index, 2) == 0
+def swap(low, high, even, axis, perms):
     inner_perm, outer_perm = perms
     outer = lax.ppermute(jnp.where(even, low, high), axis, outer_perm)
     inner = lax.ppermute(jnp.where(even, high, low), axis, inner_perm)
@@ -138,120 +137,182 @@
             o_ref[pl.ds(f * 2 * MEMBERS + r, MEMBERS, stride=2), :] = post + c_ref[k:k+1, :]
 
 
+def assimilate(turn_ref, state_ref, west_ref, east_ref, south_ref, north_ref, weight_ref, sent_ref, anomaly_ref, center_ref, wide):
+    a = HALF_COURANT
+    cols = MEMBERS
+
+    def field(f, r):
+        k = 2 * f + r
+        return state_ref[k * cols:(k + 1) * cols, :]
+
+    def beside(ref, f, r, c):
+        k = (2 * f + r) * 2 + c
+        return ref[k:k + 1, :]
+
+    def place(slot, block, low, high):
+        wide[slot, 8:8 + cols, :] = block
+        wide[slot, 7:8, :] = low
+        wide[slot, 8 + cols:9 + cols, :] = high
+
+    def slope(slot):
+        return wide[slot, 9:9 + cols, :] - wide[slot, 7:7 + cols, :]
+
+    spin = [turn_ref[1], turn_ref[2]]
+    h = [field(0, 0), field(0, 1)]
+    u = [field(1, 0), field(1, 1)]
+    v = [field(2, 0), field(2, 1)]
+    for r in range(2):
+        place(4 + r, h[r], beside(west_ref, 0, r, 1), beside(east_ref, 0, r, 0))
+        place(6 + r, u[r], beside(west_ref, 1, r, 1), beside(east_ref, 1, r, 0))
+    south_h, south_v, south_mid_v, south_mid_h = (south_ref[k * cols:(k + 1) * cols, :] for k in range(4))
+    north_h, north_v, north_mid_v, north_mid_h = (north_ref[k * cols:(k + 1) * cols, :] for k in range(4))
+    south_edge = [south_ref[4 * cols + k:4 * cols + k + 1, :] for k in range(2)]
+    north_edge = [north_ref[4 * cols + k:4 * cols + k + 1, :] for k in range(2)]
+    h_below, h_above = [south_h, h[0]], [h[1], north_h]
+    v_below, v_above = [south_v, v[0]], [v[1], north_v]
+    rate_h, rate_u, rate_v, mid_h, mid_u, mid_v = [], [], [], [], [], []
+    for r in range(2):
+        rate_h.append(-a * (slope(6 + r) + (v_above[r] - v_below[r])))
+        rate_u.append(-a * slope(4 + r) + spin[r] * v[r])
+        rate_v.append(-a * (h_above[r] - h_below[r]) - spin[r] * u[r])
+        mid_h.append(h[r] + rate_h[r])
+        mid_u.append(u[r] + rate_u[r])
+        mid_v.append(v[r] + rate_v[r])
+    for r in range(2):
+        outside_h, outside_u = [], []
+        for side, ref in enumerate((west_ref, east_ref)):
+            near, far = (1, 0) if side == 0 else (0, 1)
+            inner_h = h[r][0:1, :] if side == 0 else h[r][cols - 1:cols, :]
+            inner_u = u[r][0:1, :] if side == 0 else u[r][cols - 1:cols, :]
+            sign = -a if side == 0 else a
+            own = [beside(ref, 2, 0, near), beside(ref, 2, 1, near)]
+            below = south_edge[side] if r == 0 else own[0]
+            above = own[1] if r == 0 else north_edge[side]
+            outside_h.append(
+                beside(ref, 0, r, near) + sign * (inner_u - beside(ref, 1, r, far)) - a * (above - below)
+            )
+            outside_u.append(
+                beside(ref, 1, r, near) + sign * (inner_h - beside(ref, 0, r, far)) + spin[r] * own[r]
+            )
+        place(r, mid_h[r], *outside_h)
+        place(2 + r, mid_u[r], *outside_u)
+    has_south, has_north = turn_ref[4], turn_ref[5]
+    south_mid_h = has_south * (south_mid_h - a * v[0])
+    south_mid_v = has_south * (south_mid_v - a * h[0])
+    north_mid_h = has_north * (north_mid_h + a * v[1])
+    north_mid_v = has_north * (north_mid_v + a * h[1])
+    mid_h_below, mid_h_above = [south_mid_h, mid_h[0]], [mid_h[1], north_mid_h]
+    mid_v_below, mid_v_above = [south_mid_v, mid_v[0]], [mid_v[1], north_mid_v]
+    forecast = [None] * 6
+    for r in range(2):
+        second_h = -a * (slope(2 + r) + (mid_v_above[r] - mid_v_below[r]))
+        second_u = -a * slope(r) + spin[r] * mid_v[r]
+        second_v = -a * (mid_h_above[r] - mid_h_below[r]) - spin[r] * mid_u[r]
+        forecast[r] = h[r] + 0.5 * (rate_h[r] + second_h)
+        forecast[2 + r] = u[r] + 0.5 * (rate_u[r] + second_u)
+        forecast[4 + r] = v[r] + 0.5 * (rate_v[r] + second_v)
+    share = jnp.full((8, MEMBERS), 1.0 / MEMBERS, jnp.float32)
+    push = jnp.zeros((1, MEMBERS), jnp.float32)
+    gram = jnp.zeros((MEMBERS, MEMBERS), jnp.float32)
+    for k in range(6):
+        mean = jnp.sum(forecast[k], axis=1, keepdims=True) * (1.0 / MEMBERS)
+        anomaly = forecast[k] - mean
+        anomaly_ref[k * cols:(k + 1) * cols, :] = anomaly
+        row = lax.dot_general(
+            share, forecast[k], (((1,), (1,)), ((), ())), precision=lax.Precision.HIGHEST,
+            preferred_element_type=jnp.float32,
+        )
+        center_ref[k:k + 1, :] = row[0:1, :]
+        weight = weight_ref[k * cols:(k + 1) * cols, 0:1]
+        pull = weight_ref[k * cols:(k + 1) * cols, 1:2] - weight * mean
+        push = push + jnp.sum(pull * anomaly, axis=0, keepdims=True)
+        gram = gram + lax.dot_general(
+            weight * anomaly, anomaly, (((0,), (0,)), ((), ())), precision=lax.Precision.HIGHEST,
+            preferred_element_type=jnp.float32,
+        )
+    row_at = lax.broadcasted_iota(jnp.int32, (MEMBERS, MEMBERS), 0)
+    col_at = lax.broadcasted_iota(jnp.int32, (MEMBERS, MEMBERS), 1)
+    sent = jnp.where((row_at == MEMBERS - 1) & (col_at < MEMBERS - 1), push, gram)
+    sent_ref[...] = jnp.where((row_at == MEMBERS - 2) & (col_at == 0), push[:, MEMBERS - 1:], sent)
+
+
 def shards(prior_ensemble, observed, obs_error, obs_index, obs_count):
     a = HALF_COURANT
-    state = prior_ensemble.astype(jnp.float32)
-    members, rows, cols = state.shape[1:]
+    members, rows, cols = prior_ensemble.shape[1:]
+    entries = 3 * rows * cols
     lat_index, lon_index = lax.axis_index(LAT), lax.axis_index(LON)
     lat_count, lon_count = lax.axis_size(LAT), lax.axis_size(LON)
     lat_perms = pair_perms(lat_count, False)
     lon_perms = pair_perms(lon_count, True)
+    lat_even, lon_even = lax.rem(lat_index, 2) == 0, lax.rem(lon_index, 2) == 0
     total_rows = rows * lat_count
-    f = rotation_at(lat_index * rows - 1 + jnp.arange(4, dtype=jnp.int32), total_rows)
+    turn = rotation_at(lat_index * rows - 1 + jnp.arange(4, dtype=jnp.int32), total_rows)
     has_south = (lat_index > 0).astype(jnp.float32)
     has_north = (lat_index < lat_count - 1).astype(jnp.float32)
 
+    state = jnp.transpose(prior_ensemble, (0, 2, 3, 1)).astype(jnp.float32)
+    west, east = swap(state[:, :, :2], state[:, :, -2:], lon_even, LON, lon_perms)
+
+    inner_perm, outer_perm = lat_perms
     h, u, v = state[0], state[1], state[2]
-    zero = jnp.zeros((members, 1), jnp.float32)
-
-    def slope(row):
-        row = jnp.concatenate([zero, row, zero], axis=1)
-        return row[:, 2:] - row[:, :-2]
-
-    down = jnp.stack([
-        h[:, 0], v[:, 0],
-        h[:, 0] - a * slope(u[:, 0]) - a * v[:, 1],
-        v[:, 0] - a * h[:, 1] - f[1] * u[:, 0],
-    ])
-    up = jnp.stack([
-        h[:, 1], v[:, 1],
-        h[:, 1] - a * slope(u[:, 1]) + a * v[:, 0],
-        v[:, 1] + a * h[:, 0] - f[2] * u[:, 1],
-    ])
-    down, up, edge = lax.optimization_barrier((down, up, state))
-    south, north = swap(down, up, lat_index, LAT, lat_perms)
-
-    edge = jnp.transpose(edge, (0, 2, 3, 1))
-    west, east = swap(edge[:, :, :2], edge[:, :, -2:], lon_index, LON, lon_perms)
-
-    def corner(row):
-        return jnp.stack([west[1, row, 1], east[1, row, 0], west[2, row, 1], east[2, row, 0]])
-
-    south_corner, north_corner = swap(corner(0), corner(1), lat_index, LAT, lat_perms)
-
-    west_t = jnp.transpose(west, (0, 3, 1, 2))
-    east_t = jnp.transpose(east, (0, 3, 1, 2))
-    wide = jnp.concatenate([west_t, state, east_t], axis=-1)
-    wh, wu, wv = wide[0], wide[1], wide[2]
-
-    def widen(row, corners):
-        return jnp.concatenate([corners[2][:, None], row, corners[3][:, None]], axis=1)
-
-    def mend(row, corners):
-        return jnp.concatenate([
-            (row[:, 0] + a * corners[0])[:, None], row[:, 1:-1],
-            (row[:, -1] - a * corners[1])[:, None]], axis=1)
-
-    south_v, north_v = widen(south[1], south_corner), widen(north[1], north_corner)
-    v_above = jnp.stack([wv[:, 1, 1:-1], north_v], axis=1)
-    v_below = jnp.stack([south_v, wv[:, 0, 1:-1]], axis=1)
-    h_above = jnp.stack([h[:, 1], north[0]], axis=1)
-    h_below = jnp.stack([south[0], h[:, 0]], axis=1)
-    spin = f[1:3, None]
-    rate_h = -a * ((wu[..., 2:] - wu[..., :-2]) + (v_above - v_below))
-    rate_u = -a * (wh[..., 2:] - wh[..., :-2]) + spin * wv[..., 1:-1]
-    rate_v = -a * (h_above - h_below) - spin * u
-    mid_h = wh[..., 1:-1] + rate_h
-    mid_u = wu[..., 1:-1] + rate_u
-    mid_v = v + rate_v
-    south_mid_h = has_south * (mend(south[2], south_corner) - a * v[:, 0])
-    south_mid_v = has_south * (south[3] - a * h[:, 0])
-    north_mid_h = has_north * (mend(north[2], north_corner) + a * v[:, 1])
-    north_mid_v = has_north * (north[3] + a * h[:, 1])
-    mid_v_above = jnp.stack([mid_v[:, 1], north_mid_v], axis=1)
-    mid_v_below = jnp.stack([south_mid_v, mid_v[:, 0]], axis=1)
-    mid_h_above = jnp.stack([mid_h[:, 1, 1:-1], north_mid_h], axis=1)
-    mid_h_below = jnp.stack([south_mid_h, mid_h[:, 0, 1:-1]], axis=1)
-    second_h = -a * ((mid_u[..., 2:] - mid_u[..., :-2]) + (mid_v_above - mid_v_below))
-    second_u = -a * (mid_h[..., 2:] - mid_h[..., :-2]) + spin * mid_v
-    second_v = -a * (mid_h_above - mid_h_below) - spin * mid_u[..., 1:-1]
-    forecast = jnp.stack([
-        h + 0.5 * (rate_h[..., 1:-1] + second_h),
-        u + 0.5 * (rate_u[..., 1:-1] + second_u),
-        v + 0.5 * (rate_v + second_v),
-    ])
-
-    center = jnp.mean(forecast, axis=1, keepdims=True)
-    anomaly = forecast - center
+
+    def early(row, other, sign, spin):
+        return jnp.concatenate([h[row], v[row], v[row] + sign * a * h[other] - spin * u[row]])
+
+    down_early, up_early = early(0, 1, -1.0, turn[1]), early(1, 0, 1.0, turn[2])
+    outer_early = lax.ppermute(jnp.where(lat_even, down_early, up_early), LAT, outer_perm)
+
+    def late(row, other, sign):
+        around = jnp.concatenate([west[1, row, 1:], u[row], east[1, row, :1]])
+        mid = h[row] - a * (around[2:] - around[:-2]) + sign * a * v[other]
+        return jnp.concatenate([mid, west[2, row, 1:], east[2, row, :1]])
+
+    down_late, up_late = late(0, 1, -1.0), late(1, 0, 1.0)
+    outer_late = lax.ppermute(jnp.where(lat_even, down_late, up_late), LAT, outer_perm)
+    inner = lax.ppermute(
+        jnp.where(
+            lat_even, jnp.concatenate([up_early, up_late]), jnp.concatenate([down_early, down_late])
+        ),
+        LAT, inner_perm,
+    )
+    outer = jnp.concatenate([outer_early, outer_late])
+    south, north = jnp.where(lat_even, outer, inner), jnp.where(lat_even, inner, outer)
 
     index = obs_index.reshape(-1)
     slots = index.shape[0]
-    entries = 3 * rows * cols
     live = (jnp.arange(slots, dtype=jnp.int32) < obs_count.reshape(())).astype(jnp.float32)
     weight = live / obs_error.reshape(-1)
     weight = weight * weight
-    named = (index[:, None] == jnp.arange(entries, dtype=jnp.int32)[None, :]).astype(jnp.float32)
-    summed = jnp.dot(
-        jnp.stack([weight, weight * observed.reshape(-1)]), named, precision=lax.Precision.HIGHEST
-    ).reshape(2, 3, 1, rows, cols)
-    weighted = anomaly * summed[0]
-    pull = summed[1] - summed[0] * center
-    gram = jnp.einsum("fmrc,fnrc->mn", weighted, anomaly, precision=lax.Precision.HIGHEST)
-    push = jnp.einsum("frc,fnrc->n", pull[:, 0], anomaly, precision=lax.Precision.HIGHEST)
-
-    row_at = jnp.arange(members)[:, None]
-    col_at = jnp.arange(members)[None, :]
-    sent = jnp.where((row_at == members - 1) & (col_at < members - 1), push[None, :], gram)
-    sent = jnp.where((row_at == members - 2) & (col_at == 0), push[members - 1], sent)
+    named = (jnp.arange(entries, dtype=jnp.int32)[:, None] == index[None, :]).astype(jnp.float32)
+    weights = jnp.dot(
+        named, jnp.stack([weight, weight * observed.reshape(-1)], axis=1), precision=lax.Precision.HIGHEST
+    )
+    scalars = jnp.concatenate([turn, jnp.stack([has_south, has_north])])
+    vmem = pl.BlockSpec(memory_space=pltpu.VMEM)
+    sent, anomaly, center = pl.pallas_call(
+        assimilate,
+        in_specs=[pl.BlockSpec(memory_space=pltpu.SMEM)] + [vmem] * 6,
+        out_specs=[vmem] * 3,
+        out_shape=[
+            jax.ShapeDtypeStruct((members, members), jnp.float32),
+            jax.ShapeDtypeStruct((entries, members), jnp.float32),
+            jax.ShapeDtypeStruct((3 * rows, cols), jnp.float32),
+        ],
+        scratch_shapes=[pltpu.VMEM((8, cols + 16, members), jnp.float32)],
+        compiler_params=pltpu.CompilerParams(vmem_limit_bytes=16 * 1024 * 1024),
+        cost_estimate=pl.CostEstimate(flops=3 * 10**7, bytes_accessed=2 * 10**6, transcendentals=0),
+    )(
+        scalars, state.reshape(entries, members), west.reshape(-1, members), east.reshape(-1, members),
+        south, north, weights,
+    )
     total = all_sum(sent)
-    entries_first = jnp.transpose(anomaly, (0, 2, 3, 1)).reshape(entries, members)
     posterior = pl.pallas_call(
         finish,
-        out_shape=jax.ShapeDtypeStruct((3 * rows * members, cols), jnp.float32),
+        out_shape=jax.ShapeDtypeStruct((entries, cols), jnp.float32),
         scratch_shapes=[pltpu.VMEM((members, 2 * members), jnp.float32)],
         compiler_params=pltpu.CompilerParams(vmem_limit_bytes=16 * 1024 * 1024),
         cost_estimate=pl.CostEstimate(flops=3 * 10**7, bytes_accessed=10**6, transcendentals=0),
-    )(total, entries_first, center.reshape(3 * rows, cols))
+    )(total, anomaly, center)
     return posterior.reshape(3, members, rows, cols)
 
 

time: 120 us -> 110 us (0.917)
  waiting for transfers between devices: 24.5 us -> 8.06 us
  blocking collectives: 36.5 us -> 51.4 us
  starting transfers between devices: 41.9 us -> 36.1 us
  Pallas kernels: 5.9 us -> 7.81 us
  matrix products: 2.26 us -> 0.45 us
  local copies, waits for them, and re-layouts: 4.6 us -> 3.23 us
    ppermute x0 -> x3, starting transfers between devices: none -> 18.1 us  [the longest x1 9 us: shards(): lax.ppermute(jnp.where(lat_even, down_early, up_early), LAT, outer_perm)]
    ppermute x3 -> x1, waiting for transfers between devices: 17.1 us -> 0.01 us  [swap(): outer = lax.ppermute(jnp.where(even, low, high), axis, outer_perm)]
    all_to_all x0 -> x1, blocking collectives: none -> 12.3 us  [all_sum(): lax.all_to_all(jnp.broadcast_to(mine[None], (plane, part, cols)), PLANE,...]
    ppermute x3 -> x1, starting transfers between devices: 12.6 us -> 1.92 us  [swap(): inner = lax.ppermute(jnp.where(even, high, low), axis, inner_perm)]
    ppermute x0 -> x3, waiting for transfers between devices: none -> 8.05 us  [the longest x1 6.86 us: shards(): lax.ppermute(jnp.where(lat_even, down_early, up_early), LAT, outer_perm)]
    ppermute x3 -> x1, starting transfers between devices: 24 us -> 16.2 us  [swap(): outer = lax.ppermute(jnp.where(even, low, high), axis, outer_perm)]
    all_to_all x1 -> x0, waiting for transfers between devices: 7.34 us -> none  [all_sum(): lax.all_to_all(jnp.broadcast_to(mine[None], (plane, part, cols)), PLANE,...]
    all_to_all x1 -> x0, starting transfers between devices: 5.28 us -> none  [all_sum(): lax.all_to_all(jnp.broadcast_to(mine[None], (plane, part, cols)), PLANE,...]
  transfers between devices with their start and end apart: 7 -> 5, of which waited for: 3 -> 2; matrix products, arithmetic and copies ran while one was open for 1% -> 2% of each run, Pallas kernels for 0% -> 0%
where the time goes in v3:
time: 110 us
  blocking collectives  51.4 us (47%)
  starting transfers between devices  36.1 us (33%)
  waiting for transfers between devices  8.06 us (7%)
  Pallas kernels  7.81 us (7%)
  local copies, waits for them, and re-layouts  3.23 us (3%)
  other arithmetic  1.77 us (2%)
    all_to_all x1, blocking collectives, all_sum(): lax.all_to_all(block.reshape(plane, part, cols), PLANE, 0, 0, tiled=True)  21.7 us
    all_to_all x1, blocking collectives, all_sum(): lax.all_to_all(jnp.broadcast_to(mine[None], (line, part, cols)), LINE, 0,...  17.3 us
    ppermute x1, starting transfers between devices, swap(): outer = lax.ppermute(jnp.where(even, low, high), axis, outer_perm)  16.2 us
    all_to_all x1, blocking collectives, all_sum(): lax.all_to_all(jnp.broadcast_to(mine[None], (plane, part, cols)), PLANE,...  12.3 us
    ppermute x1, starting transfers between devices, shards(): lax.ppermute(jnp.where(lat_even, down_early, up_early), LAT, outer_perm)  9 us
    ppermute x1, starting transfers between devices, shards(): lax.ppermute(jnp.where(lat_even, down_late, up_late), LAT, outer_perm)  7.15 us
    ppermute x1, waiting for transfers between devices, shards(): lax.ppermute(jnp.where(lat_even, down_early, up_early), LAT, outer_perm)  6.86 us
    pallas_call x1, Pallas kernels, shards(): pl.pallas_call(finish, out_shape=jax.ShapeDtypeStruct((entries, cols), jn...  5.91 us
  transfers between devices with their start and end apart: 5, of which 2 were waited for; matrix products, arithmetic and copies ran while one was open for 2% of the time, Pallas kernels for 0%

profile of v3, /device:TPU:1, one launch (start us, length us, event | category | flops | bytes accessed | tf_op | source)
XLA Modules:
  0.0 109.7 jit_solution(17428383260824355323)
XLA Ops:
  0.0 1.1 %copy.12 = bf16[3,128,2,128]{1,3,2,0:T(8,128)(2,1)S(1)} copy(bf16[3,128,2,128]{3,2,1,0:T(2,128)(2,1)} %param.5) | data formatting | bytes 393216 | tf_op args[0]
  1.1 0.1 convert_bitcast_fusion
  1.2 16.2 %collective-permute-start = (f32[3,2,2,128]{3,2,1,0:T(2,128)S(1)}, f32[3,2,2,128]{3,2,1,0:T(2,128)S(1)}, u32[]{:S(2)}, u32[]{:S(2)}) collective-permute-start(f32[3,2,2,128]{3,2,1,0:T(2,128)S(1)} %get-tuple-element.25), channel_id=1, source_target_pairs={{1,2},{2,1},{3,4},{4,3},{5,6},{6,5},{7,8},{8,7},{9,10},{10,9},{11,... | collective-permute-start | bytes 18440 | tf_op jit(solution)/shard_map/ppermute | solution.py:38
  17.4 1.9 %collective-permute-start.1 = (f32[3,2,2,128]{3,2,1,0:T(2,128)S(1)}, f32[3,2,2,128]{3,2,1,0:T(2,128)S(1)}, u32[]{:S(2)}, u32[]{:S(2)}) collective-permute-start(f32[3,2,2,128]{3,2,1,0:T(2,128)S(1)} %get-tuple-element.24), channel_id=1, source_target_pairs={{0,1},{1,0},{2,3},{3,2},{4,5},{5,4},{6,7},{7,6},{8,9},{9,8},{10,11... | collective-permute-start | bytes 18440 | tf_op jit(solution)/shard_map/ppermute | solution.py:39
  19.4 0.6 fusion.17
  20.0 0.0 copy-start.2
  20.0 0.7 multiply_subtract_fusion.1
  21.3 0.0 copy-start.1
  21.4 0.0 copy-done.2
  21.4 0.7 copy-done.1
  22.0 0.0 copy-start
  22.0 0.7 copy-done
  22.7 0.5 fusion.weight_ref
  23.2 0.1 pad_maximum_fusion.4.turn_ref
  23.3 0.0 collective-permute-done
  23.3 0.0 collective-permute-done.1
  23.3 0.7 fusion.5
  24.0 9.0 %collective-permute-start.2 = (f32[384,128]{1,0:T(8,128)S(1)}, f32[384,128]{1,0:T(8,128)S(1)}, u32[]{:S(2)}, u32[]{:S(2)}) collective-permute-start(f32[384,128]{1,0:T(8,128)S(1)} %maximum_select_fusion), channel_id=1, source_target_pairs={{32,64},{64,32},{96,128},{128,96},{160,192},{192,160},{224,256},{2... | collective-permute-start | bytes 589832 | tf_op jit(solution)/shard_map/ppermute | solution.py:263
  33.1 1.9 %collective-permute-start.4 = (f32[514,128]{1,0:T(8,128)S(1)}, f32[514,128]{1,0:T(8,128)S(1)}, u32[]{:S(2)}, u32[]{:S(2)}) collective-permute-start(f32[514,128]{1,0:T(8,128)S(1)} %broadcast_select_fusion.2), channel_id=1, source_target_pairs={{0,32},{32,0},{64,96},{96,64},{128,160},{160,128},{192,224},{224,1... | collective-permute-start | bytes 789512 | tf_op jit(solution)/shard_map/ppermute | solution.py:272
  35.1 7.2 %collective-permute-start.3 = (f32[130,128]{1,0:T(8,128)S(1)}, f32[130,128]{1,0:T(8,128)S(1)}, u32[]{:S(2)}, u32[]{:S(2)}) collective-permute-start(f32[130,128]{1,0:T(8,128)S(1)} %maximum_select_fusion.1), channel_id=1, source_target_pairs={{32,64},{64,32},{96,128},{128,96},{160,192},{192,160},{224,256},{2... | collective-permute-start | bytes 199688 | tf_op jit(solution)/shard_map/ppermute | solution.py:271
  42.3 6.9 %collective-permute-done.2 = f32[384,128]{1,0:T(8,128)S(1)} collective-permute-done((f32[384,128]{1,0:T(8,128)S(1)}, f32[384,128]{1,0:T(8,128)S(1)}, u32[]{:S(2)}, u32[]{:S(2)}) %collective-permute-start.2) | collective-permute-done | bytes 196640 | tf_op jit(solution)/shard_map/ppermute | solution.py:263
  49.2 1.2 %collective-permute-done.3 = f32[130,128]{1,0:T(8,128)S(1)} collective-permute-done((f32[130,128]{1,0:T(8,128)S(1)}, f32[130,128]{1,0:T(8,128)S(1)}, u32[]{:S(2)}, u32[]{:S(2)}) %collective-permute-start.3) | collective-permute-done | bytes 66592 | tf_op jit(solution)/shard_map/ppermute | solution.py:271
  50.4 0.0 collective-permute-done.4
  50.4 1.9 %shard_map.55 = (f32[128,128]{1,0:T(8,128)S(1)}, f32[768,128]{1,0:T(8,128)S(1)}, f32[6,128]{1,0:T(8,128)S(1)}) custom-call(f32[6]{0:T(128)S(1)} %pad_maximum_fusion.4.turn_ref, f32[768,128]{1,0:T(8,128)S(1)} %bitcast.67, f32[12,128]{1,0:T(8,128)S(1)} %reshape.81.west_ref, f32[12,128]{1,0:T(8,128)S(1)} %reshape.82.east_ref, ...), custom_call_target="tpu_custom_call" | custom-call | flops 30000000 | bytes 2000000 | tf_op jit(solution)/shard_map/pallas_call | solution.py:292
  52.3 21.7 %all_to_all.15 = f32[32,4,128]{2,1,0:T(4,128)S(1)} all-to-all(f32[32,4,128]{2,1,0:T(4,128)S(1)} %bitcast.69), channel_id=1, replica_groups=mesh['x'=4,'zh'=2,'core'=2,'zl'=8,'y'=4] {'x','core','y'}, dimensions={0} | all-to-all | bytes 131072 | tf_op jit(solution)/shard_map/all_to_all | solution.py:48
  74.1 17.3 %all_to_all.16 = f32[16,4,128]{2,1,0:T(4,128)S(1)} all-to-all(f32[16,4,128]{2,1,0:T(4,128)S(1)} %broadcast_in_dim.4), channel_id=1, replica_groups=mesh['x'=4,'zh'=2,'core'=2,'zl'=8,'y'=4] {'zh','zl'}, dimensions={0} | all-to-all | bytes 65536 | tf_op jit(solution)/shard_map/all_to_all | solution.py:49
  91.4 12.3 %all_to_all.17 = f32[32,4,128]{2,1,0:T(4,128)S(1)} all-to-all(f32[32,4,128]{2,1,0:T(4,128)S(1)} %broadcast_in_dim.5), channel_id=1, replica_groups=mesh['x'=4,'zh'=2,'core'=2,'zl'=8,'y'=4] {'x','core','y'}, dimensions={0} | all-to-all | bytes 131072 | tf_op jit(solution)/shard_map/all_to_all | solution.py:52
  103.8 5.9 %shard_map.56 = f32[768,128]{1,0:T(8,128)} custom-call(f32[128,128]{1,0:T(8,128)S(1)} %bitcast.68, f32[768,128]{1,0:T(8,128)S(1)} %get-tuple-element.9.x_ref, f32[6,128]{1,0:T(8,128)S(1)} %get-tuple-element.10.c_ref), custom_call_target="tpu_custom_call" | custom-call | flops 30000000 | bytes 1000000 | tf_op jit(solution)/shard_map/pallas_call | solution.py:309
  (20 shorter events, 0.4 us)
Async XLA Ops:
  1.2 22.1 %collective-permute-start = (f32[3,2,2,128]{3,2,1,0:T(2,128)S(1)}, f32[3,2,2,128]{3,2,1,0:T(2,128)S(1)}, u32[]{:S(2)}, u32[]{:S(2)}) collective-permute-start(f32[3,2,2,128]{3,2,1,0:T(2,128)S(1)} %get-tuple-element.25), channel_id=1, source_target_pairs={{1,2},{2,1},{3,4},{4,3},{5,6},{6,5},{7,8},{8,7},{9,10},{10,9},{11,... | collective-permute-start | bytes 18440 | tf_op jit(solution)/shard_map/ppermute | solution.py:38
  17.4 5.9 %collective-permute-start.1 = (f32[3,2,2,128]{3,2,1,0:T(2,128)S(1)}, f32[3,2,2,128]{3,2,1,0:T(2,128)S(1)}, u32[]{:S(2)}, u32[]{:S(2)}) collective-permute-start(f32[3,2,2,128]{3,2,1,0:T(2,128)S(1)} %get-tuple-element.24), channel_id=1, source_target_pairs={{0,1},{1,0},{2,3},{3,2},{4,5},{5,4},{6,7},{7,6},{8,9},{9,8},{10,11... | collective-permute-start | bytes 18440 | tf_op jit(solution)/shard_map/ppermute | solution.py:39
  20.0 1.4 %copy-start.2 = (f32[1,1,256]{2,1,0:T(1,128)S(1)}, f32[1,1,256]{2,1,0:T(1,128)}, u32[]{:S(2)}) copy-start(f32[1,1,256]{2,1,0:T(1,128)} %param.7) | copy-start | bytes 3076
  21.3 0.7 copy-start.1
  22.0 0.7 copy-start
  24.0 25.1 %collective-permute-start.2 = (f32[384,128]{1,0:T(8,128)S(1)}, f32[384,128]{1,0:T(8,128)S(1)}, u32[]{:S(2)}, u32[]{:S(2)}) collective-permute-start(f32[384,128]{1,0:T(8,128)S(1)} %maximum_select_fusion), channel_id=1, source_target_pairs={{32,64},{64,32},{96,128},{128,96},{160,192},{192,160},{224,256},{2... | collective-permute-start | bytes 589832 | tf_op jit(solution)/shard_map/ppermute | solution.py:263
  33.1 17.2 %collective-permute-start.4 = (f32[514,128]{1,0:T(8,128)S(1)}, f32[514,128]{1,0:T(8,128)S(1)}, u32[]{:S(2)}, u32[]{:S(2)}) collective-permute-start(f32[514,128]{1,0:T(8,128)S(1)} %broadcast_select_fusion.2), channel_id=1, source_target_pairs={{0,32},{32,0},{64,96},{96,64},{128,160},{160,128},{192,224},{224,1... | collective-permute-start | bytes 789512 | tf_op jit(solution)/shard_map/ppermute | solution.py:272
  35.1 15.2 %collective-permute-start.3 = (f32[130,128]{1,0:T(8,128)S(1)}, f32[130,128]{1,0:T(8,128)S(1)}, u32[]{:S(2)}, u32[]{:S(2)}) collective-permute-start(f32[130,128]{1,0:T(8,128)S(1)} %maximum_select_fusion.1), channel_id=1, source_target_pairs={{32,64},{64,32},{96,128},{128,96},{160,192},{192,160},{224,256},{2... | collective-permute-start | bytes 199688 | tf_op jit(solution)/shard_map/ppermute | solution.py:271

commit v4 on v3

--- a/solution.py
+++ b/solution.py
@@ -31,13 +31,6 @@
             j = (i + 1) % count
             outer += [(i, j), (j, i)]
     return inner, outer
-
-
-def swap(low, high, even, axis, perms):
-    inner_perm, outer_perm = perms
-    outer = lax.ppermute(jnp.where(even, low, high), axis, outer_perm)
-    inner = lax.ppermute(jnp.where(even, high, low), axis, inner_perm)
-    return jnp.where(even, outer, inner), jnp.where(even, inner, outer)
 
 
 def all_sum(block):
@@ -135,6 +128,80 @@
             k = 2 * f + r
             post = lax.dot_general(weights, x_ref[k * MEMBERS:(k + 1) * MEMBERS, :], (((1,), (1,)), ((), ())), precision=lax.Precision.HIGHEST, preferred_element_type=jnp.float32)
             o_ref[pl.ds(f * 2 * MEMBERS + r, MEMBERS, stride=2), :] = post + c_ref[k:k+1, :]
+
+
+def turned(even_ref, prior_ref, state_ref, outer_ref, inner_ref, rows_ref):
+    cols = MEMBERS
+    even = even_ref[0] > 0
+    for f in range(3):
+        rows_ref[...] = prior_ref[2 * cols * f:2 * cols * (f + 1), :].astype(jnp.float32)
+        for r in range(2):
+            k = 2 * f + r
+            block = rows_ref[pl.ds(r, cols, stride=2), :].T
+            state_ref[k * cols:(k + 1) * cols, :] = block
+            low, high = block[:2, :], block[cols - 2:, :]
+            outer_ref[2 * k:2 * k + 2, :] = jnp.where(even, low, high)
+            inner_ref[2 * k:2 * k + 2, :] = jnp.where(even, high, low)
+
+
+def early_rows(turn_ref, state_ref, out_ref):
+    row = turn_ref[6].astype(jnp.int32)
+    other = 1 - row
+    sign = 2.0 * turn_ref[6] - 1.0
+    spin = turn_ref[1 + row]
+    cols = MEMBERS
+
+    def field(f, r):
+        return state_ref[pl.ds(pl.multiple_of((2 * f + r) * cols, cols), cols), :]
+
+    h, v = field(0, row), field(2, row)
+    out_ref[:cols, :] = h
+    out_ref[cols:2 * cols, :] = v
+    out_ref[2 * cols:, :] = v + (sign * HALF_COURANT) * field(0, other) - spin * field(1, row)
+
+
+def edge_rows(state_ref, west_ref, east_ref, wide, row, sign):
+    cols = MEMBERS
+
+    def field(f, r):
+        return state_ref[pl.ds(pl.multiple_of((2 * f + r) * cols, cols), cols), :]
+
+    def beside(ref, f, c):
+        return ref[pl.ds((2 * f + row) * 2 + c, 1), :]
+
+    wide[8:8 + cols, :] = field(1, row)
+    wide[7:8, :] = beside(west_ref, 1, 1)
+    wide[8 + cols:9 + cols, :] = beside(east_ref, 1, 0)
+    slope = wide[9:9 + cols, :] - wide[7:7 + cols, :]
+    mid = field(0, row) - HALF_COURANT * slope + (sign * HALF_COURANT) * field(2, 1 - row)
+    return field, mid, beside(west_ref, 2, 1), beside(east_ref, 2, 0)
+
+
+def late_rows(turn_ref, state_ref, west_ref, east_ref, out_ref, wide):
+    cols = MEMBERS
+    row = turn_ref[6].astype(jnp.int32)
+    _, mid, west_v, east_v = edge_rows(
+        state_ref, west_ref, east_ref, wide, row, 2.0 * turn_ref[6] - 1.0
+    )
+    out_ref[:cols, :] = mid
+    out_ref[cols:cols + 1, :] = west_v
+    out_ref[cols + 1:cols + 2, :] = east_v
+
+
+def inner_rows(turn_ref, state_ref, west_ref, east_ref, out_ref, wide):
+    cols = MEMBERS
+    row = 1 - turn_ref[6].astype(jnp.int32)
+    sign = 1.0 - 2.0 * turn_ref[6]
+    field, mid, west_v, east_v = edge_rows(state_ref, west_ref, east_ref, wide, row, sign)
+    h, v = field(0, row), field(2, row)
+    out_ref[:cols, :] = h
+    out_ref[cols:2 * cols, :] = v
+    out_ref[2 * cols:3 * cols, :] = (
+        v + (sign * HALF_COURANT) * field(0, 1 - row) - turn_ref[1 + row] * field(1, row)
+    )
+    out_ref[3 * cols:4 * cols, :] = mid
+    out_ref[4 * cols:4 * cols + 1, :] = west_v
+    out_ref[4 * cols + 1:4 * cols + 2, :] = east_v
 
 
 def assimilate(turn_ref, state_ref, west_ref, east_ref, south_ref, north_ref, weight_ref, sent_ref, anomaly_ref, center_ref, wide):
@@ -250,31 +317,55 @@
     has_south = (lat_index > 0).astype(jnp.float32)
     has_north = (lat_index < lat_count - 1).astype(jnp.float32)
 
-    state = jnp.transpose(prior_ensemble, (0, 2, 3, 1)).astype(jnp.float32)
-    west, east = swap(state[:, :, :2], state[:, :, -2:], lon_even, LON, lon_perms)
+    smem = pl.BlockSpec(memory_space=pltpu.SMEM)
+    vmem = pl.BlockSpec(memory_space=pltpu.VMEM)
+    params = pltpu.CompilerParams(vmem_limit_bytes=16 * 1024 * 1024)
+    edges = 2 * 3 * rows
+    state, outer_edge, inner_edge = pl.pallas_call(
+        turned,
+        in_specs=[smem, vmem],
+        out_specs=[vmem] * 3,
+        out_shape=[
+            jax.ShapeDtypeStruct((entries, members), jnp.float32),
+            jax.ShapeDtypeStruct((edges, members), jnp.float32),
+            jax.ShapeDtypeStruct((edges, members), jnp.float32),
+        ],
+        scratch_shapes=[pltpu.VMEM((rows * members, cols), jnp.float32)],
+        compiler_params=params,
+        cost_estimate=pl.CostEstimate(flops=10**5, bytes_accessed=6 * 10**5, transcendentals=0),
+    )(lon_even.astype(jnp.int32).reshape(1), prior_ensemble.reshape(entries, cols))
+    lon_inner, lon_outer = lon_perms
+    outer_edge = lax.ppermute(outer_edge, LON, lon_outer)
+    inner_edge = lax.ppermute(inner_edge, LON, lon_inner)
+    west = jnp.where(lon_even, outer_edge, inner_edge)
+    east = jnp.where(lon_even, inner_edge, outer_edge)
 
     inner_perm, outer_perm = lat_perms
-    h, u, v = state[0], state[1], state[2]
-
-    def early(row, other, sign, spin):
-        return jnp.concatenate([h[row], v[row], v[row] + sign * a * h[other] - spin * u[row]])
-
-    down_early, up_early = early(0, 1, -1.0, turn[1]), early(1, 0, 1.0, turn[2])
-    outer_early = lax.ppermute(jnp.where(lat_even, down_early, up_early), LAT, outer_perm)
-
-    def late(row, other, sign):
-        around = jnp.concatenate([west[1, row, 1:], u[row], east[1, row, :1]])
-        mid = h[row] - a * (around[2:] - around[:-2]) + sign * a * v[other]
-        return jnp.concatenate([mid, west[2, row, 1:], east[2, row, :1]])
-
-    down_late, up_late = late(0, 1, -1.0), late(1, 0, 1.0)
-    outer_late = lax.ppermute(jnp.where(lat_even, down_late, up_late), LAT, outer_perm)
-    inner = lax.ppermute(
-        jnp.where(
-            lat_even, jnp.concatenate([up_early, up_late]), jnp.concatenate([down_early, down_late])
-        ),
-        LAT, inner_perm,
-    )
+    edge_row = 1.0 - lat_even.astype(jnp.float32)
+    scalars = jnp.concatenate([turn, jnp.stack([has_south, has_north, edge_row])])
+    outer_early = pl.pallas_call(
+        early_rows,
+        in_specs=[smem, vmem],
+        out_specs=vmem,
+        out_shape=jax.ShapeDtypeStruct((3 * cols, members), jnp.float32),
+        compiler_params=params,
+        cost_estimate=pl.CostEstimate(flops=10**5, bytes_accessed=10**5, transcendentals=0),
+    )(scalars, state)
+    outer_early = lax.ppermute(outer_early, LAT, outer_perm)
+
+    def edge_call(kernel, height):
+        return pl.pallas_call(
+            kernel,
+            in_specs=[smem] + [vmem] * 3,
+            out_specs=vmem,
+            out_shape=jax.ShapeDtypeStruct((height, members), jnp.float32),
+            scratch_shapes=[pltpu.VMEM((cols + 16, members), jnp.float32)],
+            compiler_params=params,
+            cost_estimate=pl.CostEstimate(flops=10**5, bytes_accessed=10**5, transcendentals=0),
+        )(scalars, state, west, east)
+
+    outer_late = lax.ppermute(edge_call(late_rows, cols + 2), LAT, outer_perm)
+    inner = lax.ppermute(edge_call(inner_rows, 4 * cols + 2), LAT, inner_perm)
     outer = jnp.concatenate([outer_early, outer_late])
     south, north = jnp.where(lat_even, outer, inner), jnp.where(lat_even, inner, outer)
 
@@ -287,11 +378,9 @@
     weights = jnp.dot(
         named, jnp.stack([weight, weight * observed.reshape(-1)], axis=1), precision=lax.Precision.HIGHEST
     )
-    scalars = jnp.concatenate([turn, jnp.stack([has_south, has_north])])
-    vmem = pl.BlockSpec(memory_space=pltpu.VMEM)
     sent, anomaly, center = pl.pallas_call(
         assimilate,
-        in_specs=[pl.BlockSpec(memory_space=pltpu.SMEM)] + [vmem] * 6,
+        in_specs=[smem] + [vmem] * 6,
         out_specs=[vmem] * 3,
         out_shape=[
             jax.ShapeDtypeStruct((members, members), jnp.float32),
@@ -299,18 +388,17 @@
             jax.ShapeDtypeStruct((3 * rows, cols), jnp.float32),
         ],
         scratch_shapes=[pltpu.VMEM((8, cols + 16, members), jnp.float32)],
-        compiler_params=pltpu.CompilerParams(vmem_limit_bytes=16 * 1024 * 1024),
+        compiler_params=params,
         cost_estimate=pl.CostEstimate(flops=3 * 10**7, bytes_accessed=2 * 10**6, transcendentals=0),
     )(
-        scalars, state.reshape(entries, members), west.reshape(-1, members), east.reshape(-1, members),
-        south, north, weights,
+        scalars, state, west, east, south, north, weights,
     )
     total = all_sum(sent)
     posterior = pl.pallas_call(
         finish,
         out_shape=jax.ShapeDtypeStruct((entries, cols), jnp.float32),
         scratch_shapes=[pltpu.VMEM((members, 2 * members), jnp.float32)],
-        compiler_params=pltpu.CompilerParams(vmem_limit_bytes=16 * 1024 * 1024),
+        compiler_params=params,
         cost_estimate=pl.CostEstimate(flops=3 * 10**7, bytes_accessed=10**6, transcendentals=0),
     )(total, anomaly, center)
     return posterior.reshape(3, members, rows, cols)

time: 110 us -> 107 us (0.973)
  blocking collectives: 51.4 us -> 49.5 us
  Pallas kernels: 7.81 us -> 9.69 us
  other arithmetic: 1.77 us -> 0.25 us
    all_to_all x1, blocking collectives: 21.7 us -> 18.5 us  [all_sum(): lax.all_to_all(block.reshape(plane, part, cols), PLANE, 0, 0, tiled=True)]
    pallas_call x1 -> x5, Pallas kernels: 1.9 us -> 3.78 us  [the longest x1 1.9 us: shards(): pl.pallas_call(assimilate, in_specs=[smem] + [vmem] * 6, out_specs=[vmem]...]
    all_to_all x1, blocking collectives: 17.3 us -> 18.6 us  [all_sum(): lax.all_to_all(jnp.broadcast_to(mine[None], (line, part, cols)), LINE, 0,...]
    unnamed x8 -> x9, local copies, waits for them, and re-layouts: 2.46 us -> 2.28 us
  transfers between devices with their start and end apart: 5 -> 5, of which waited for: 2 -> 2; matrix products, arithmetic and copies ran while one was open for 2% -> 1% of each run, Pallas kernels for 0% -> 2%
where the time goes in v4:
time: 107 us; the launch traced here: 106 us
  blocking collectives  49.5 us (46%)
  starting transfers between devices  36.1 us (34%)
  Pallas kernels  9.69 us (9%)
  waiting for transfers between devices  7.04 us (7%)
  local copies, waits for them, and re-layouts  2.31 us (2%)
    all_to_all x1, blocking collectives, all_sum(): lax.all_to_all(jnp.broadcast_to(mine[None], (line, part, cols)), LINE, 0,...  18.6 us
    all_to_all x1, blocking collectives, all_sum(): lax.all_to_all(block.reshape(plane, part, cols), PLANE, 0, 0, tiled=True)  18.5 us
    ppermute x1, starting transfers between devices, shards(): outer_edge = lax.ppermute(outer_edge, LON, lon_outer)  16.2 us
    all_to_all x1, blocking collectives, all_sum(): lax.all_to_all(jnp.broadcast_to(mine[None], (plane, part, cols)), PLANE,...  12.3 us
    ppermute x1, starting transfers between devices, shards(): outer_early = lax.ppermute(outer_early, LAT, outer_perm)  8.78 us
    ppermute x1, starting transfers between devices, shards(): outer_late = lax.ppermute(edge_call(late_rows, cols + 2), LAT, outer_perm)  7.37 us
    pallas_call x1, Pallas kernels, shards(): pl.pallas_call(finish, out_shape=jax.ShapeDtypeStruct((entries, cols), jn...  5.91 us
    ppermute x1, waiting for transfers between devices, shards(): outer_late = lax.ppermute(edge_call(late_rows, cols + 2), LAT, outer_perm)  5.29 us
  transfers between devices with their start and end apart: 5, of which 2 were waited for; matrix products, arithmetic and copies ran while one was open for 1% of the time, Pallas kernels for 2%

profile of v4, /device:TPU:1, one launch (start us, length us, event | category | flops | bytes accessed | tf_op | source)
XLA Modules:
  0.0 106.2 jit_solution(15068882529349522104)
XLA Ops:
  0.0 0.0 copy-start
  0.0 0.9 copy-done
  0.9 0.1 shard_map.55
  1.1 16.2 %collective-permute-start = (f32[12,128]{1,0:T(8,128)S(1)}, f32[12,128]{1,0:T(8,128)S(1)}, u32[]{:S(2)}, u32[]{:S(2)}) collective-permute-start(f32[12,128]{1,0:T(8,128)S(1)} %get-tuple-element.12), channel_id=1, source_target_pairs={{1,2},{2,1},{3,4},{4,3},{5,6},{6,5},{7,8},{8,7},{9,10},{10,9},{11,... | collective-permute-start | bytes 18440 | tf_op jit(solution)/shard_map/ppermute | solution.py:338
  17.2 1.9 %collective-permute-start.1 = (f32[12,128]{1,0:T(8,128)S(1)}, f32[12,128]{1,0:T(8,128)S(1)}, u32[]{:S(2)}, u32[]{:S(2)}) collective-permute-start(f32[12,128]{1,0:T(8,128)S(1)} %get-tuple-element.13), channel_id=1, source_target_pairs={{0,1},{1,0},{2,3},{3,2},{4,5},{5,4},{6,7},{7,6},{8,9},{9,8},{10,11... | collective-permute-start | bytes 18440 | tf_op jit(solution)/shard_map/ppermute | solution.py:339
  19.3 0.1 pad_maximum_fusion.turn_ref
  19.3 0.0 copy-start.3
  19.3 0.6 shard_map.56
  19.9 8.8 %collective-permute-start.2 = (f32[384,128]{1,0:T(8,128)S(1)}, f32[384,128]{1,0:T(8,128)S(1)}, u32[]{:S(2)}, u32[]{:S(2)}) collective-permute-start(f32[384,128]{1,0:T(8,128)S(1)} %shard_map.56), channel_id=1, source_target_pairs={{32,64},{64,32},{96,128},{128,96},{160,192},{192,160},{224,256},{2... | collective-permute-start | bytes 589832 | tf_op jit(solution)/shard_map/ppermute | solution.py:354
  29.3 0.0 copy-start.2
  29.4 0.0 copy-done.3
  29.4 0.7 copy-done.2
  30.0 0.0 collective-permute-done
  30.1 0.0 collective-permute-done.1
  30.1 0.6 shard_map.58
  30.7 1.9 %collective-permute-start.4 = (f32[514,128]{1,0:T(8,128)S(1)}, f32[514,128]{1,0:T(8,128)S(1)}, u32[]{:S(2)}, u32[]{:S(2)}) collective-permute-start(f32[514,128]{1,0:T(8,128)S(1)} %shard_map.58), channel_id=1, source_target_pairs={{0,32},{32,0},{64,96},{96,64},{128,160},{160,128},{192,224},{224,1... | collective-permute-start | bytes 789512 | tf_op jit(solution)/shard_map/ppermute | solution.py:368
  32.6 0.0 copy-start.1
  32.6 0.7 copy-done.1
  33.3 0.5 fusion.weight_ref
  33.7 0.6 shard_map.57
  34.3 7.4 %collective-permute-start.3 = (f32[130,128]{1,0:T(8,128)S(1)}, f32[130,128]{1,0:T(8,128)S(1)}, u32[]{:S(2)}, u32[]{:S(2)}) collective-permute-start(f32[130,128]{1,0:T(8,128)S(1)} %shard_map.57), channel_id=1, source_target_pairs={{32,64},{64,32},{96,128},{128,96},{160,192},{192,160},{224,256},{2... | collective-permute-start | bytes 199688 | tf_op jit(solution)/shard_map/ppermute | solution.py:367
  41.7 1.7 %collective-permute-done.2 = f32[384,128]{1,0:T(8,128)S(1)} collective-permute-done((f32[384,128]{1,0:T(8,128)S(1)}, f32[384,128]{1,0:T(8,128)S(1)}, u32[]{:S(2)}, u32[]{:S(2)}) %collective-permute-start.2) | collective-permute-done | bytes 196640 | tf_op jit(solution)/shard_map/ppermute | solution.py:354
  43.5 5.3 %collective-permute-done.3 = f32[130,128]{1,0:T(8,128)S(1)} collective-permute-done((f32[130,128]{1,0:T(8,128)S(1)}, f32[130,128]{1,0:T(8,128)S(1)}, u32[]{:S(2)}, u32[]{:S(2)}) %collective-permute-start.3) | collective-permute-done | bytes 66592 | tf_op jit(solution)/shard_map/ppermute | solution.py:367
  48.8 0.0 collective-permute-done.4
  48.8 1.9 %shard_map.59 = (f32[128,128]{1,0:T(8,128)S(1)}, f32[768,128]{1,0:T(8,128)S(1)}, f32[6,128]{1,0:T(8,128)S(1)}) custom-call(f32[7]{0:T(128)S(1)} %pad_maximum_fusion.turn_ref, f32[768,128]{1,0:T(8,128)S(1)} %get-tuple-element.11.state_ref, f32[12,128]{1,0:T(8,128)S(1)} %get-tuple-element.22.west_ref, f32[12,128]{1,0:T(8,128)S(1)} %get-tuple-element.21.east_ref, ...), custom_call_target="tpu_custom_call" | custom-call | flops 30000000 | bytes 2000000 | tf_op jit(solution)/shard_map/pallas_call | solution.py:381
  50.7 18.5 %all_to_all.15 = f32[32,4,128]{2,1,0:T(4,128)S(1)} all-to-all(f32[32,4,128]{2,1,0:T(4,128)S(1)} %bitcast.18), channel_id=1, replica_groups=mesh['x'=4,'zh'=2,'core'=2,'zl'=8,'y'=4] {'x','core','y'}, dimensions={0} | all-to-all | bytes 131072 | tf_op jit(solution)/shard_map/all_to_all | solution.py:41
  69.3 18.6 %all_to_all.16 = f32[16,4,128]{2,1,0:T(4,128)S(1)} all-to-all(f32[16,4,128]{2,1,0:T(4,128)S(1)} %broadcast_in_dim.4), channel_id=1, replica_groups=mesh['x'=4,'zh'=2,'core'=2,'zl'=8,'y'=4] {'zh','zl'}, dimensions={0} | all-to-all | bytes 65536 | tf_op jit(solution)/shard_map/all_to_all | solution.py:42
  87.9 12.3 %all_to_all.17 = f32[32,4,128]{2,1,0:T(4,128)S(1)} all-to-all(f32[32,4,128]{2,1,0:T(4,128)S(1)} %broadcast_in_dim.5), channel_id=1, replica_groups=mesh['x'=4,'zh'=2,'core'=2,'zl'=8,'y'=4] {'x','core','y'}, dimensions={0} | all-to-all | bytes 131072 | tf_op jit(solution)/shard_map/all_to_all | solution.py:45
  100.3 5.9 %shard_map.60 = f32[768,128]{1,0:T(8,128)} custom-call(f32[128,128]{1,0:T(8,128)S(1)} %bitcast.16, f32[768,128]{1,0:T(8,128)S(1)} %get-tuple-element.15.x_ref, f32[6,128]{1,0:T(8,128)S(1)} %get-tuple-element.16.c_ref), custom_call_target="tpu_custom_call" | custom-call | flops 30000000 | bytes 1000000 | tf_op jit(solution)/shard_map/pallas_call | solution.py:397
  (10 shorter events, 0.2 us)
Async XLA Ops:
  0.0 0.9 copy-start
  1.1 29.0 %collective-permute-start = (f32[12,128]{1,0:T(8,128)S(1)}, f32[12,128]{1,0:T(8,128)S(1)}, u32[]{:S(2)}, u32[]{:S(2)}) collective-permute-start(f32[12,128]{1,0:T(8,128)S(1)} %get-tuple-element.12), channel_id=1, source_target_pairs={{1,2},{2,1},{3,4},{4,3},{5,6},{6,5},{7,8},{8,7},{9,10},{10,9},{11,... | collective-permute-start | bytes 18440 | tf_op jit(solution)/shard_map/ppermute | solution.py:338
  17.2 12.8 %collective-permute-start.1 = (f32[12,128]{1,0:T(8,128)S(1)}, f32[12,128]{1,0:T(8,128)S(1)}, u32[]{:S(2)}, u32[]{:S(2)}) collective-permute-start(f32[12,128]{1,0:T(8,128)S(1)} %get-tuple-element.13), channel_id=1, source_target_pairs={{0,1},{1,0},{2,3},{3,2},{4,5},{5,4},{6,7},{7,6},{8,9},{9,8},{10,11... | collective-permute-start | bytes 18440 | tf_op jit(solution)/shard_map/ppermute | solution.py:339
  19.3 10.0 %copy-start.3 = (f32[1,1,256]{2,1,0:T(1,128)S(1)}, f32[1,1,256]{2,1,0:T(1,128)}, u32[]{:S(2)}) copy-start(f32[1,1,256]{2,1,0:T(1,128)} %param.7) | copy-start | bytes 3076
  19.9 23.5 %collective-permute-start.2 = (f32[384,128]{1,0:T(8,128)S(1)}, f32[384,128]{1,0:T(8,128)S(1)}, u32[]{:S(2)}, u32[]{:S(2)}) collective-permute-start(f32[384,128]{1,0:T(8,128)S(1)} %shard_map.56), channel_id=1, source_target_pairs={{32,64},{64,32},{96,128},{128,96},{160,192},{192,160},{224,256},{2... | collective-permute-start | bytes 589832 | tf_op jit(solution)/shard_map/ppermute | solution.py:354
  29.3 0.7 copy-start.2
  30.7 18.1 %collective-permute-start.4 = (f32[514,128]{1,0:T(8,128)S(1)}, f32[514,128]{1,0:T(8,128)S(1)}, u32[]{:S(2)}, u32[]{:S(2)}) collective-permute-start(f32[514,128]{1,0:T(8,128)S(1)} %shard_map.58), channel_id=1, source_target_pairs={{0,32},{32,0},{64,96},{96,64},{128,160},{160,128},{192,224},{224,1... | collective-permute-start | bytes 789512 | tf_op jit(solution)/shard_map/ppermute | solution.py:368
  32.6 0.7 copy-start.1
  34.3 14.4 %collective-permute-start.3 = (f32[130,128]{1,0:T(8,128)S(1)}, f32[130,128]{1,0:T(8,128)S(1)}, u32[]{:S(2)}, u32[]{:S(2)}) collective-permute-start(f32[130,128]{1,0:T(8,128)S(1)} %shard_map.57), channel_id=1, source_target_pairs={{32,64},{64,32},{96,128},{128,96},{160,192},{192,160},{224,256},{2... | collective-permute-start | bytes 199688 | tf_op jit(solution)/shard_map/ppermute | solution.py:367

commit v5 on v3

--- a/solution.py
+++ b/solution.py
@@ -31,13 +31,6 @@
             j = (i + 1) % count
             outer += [(i, j), (j, i)]
     return inner, outer
-
-
-def swap(low, high, even, axis, perms):
-    inner_perm, outer_perm = perms
-    outer = lax.ppermute(jnp.where(even, low, high), axis, outer_perm)
-    inner = lax.ppermute(jnp.where(even, high, low), axis, inner_perm)
-    return jnp.where(even, outer, inner), jnp.where(even, inner, outer)
 
 
 def all_sum(block):
@@ -137,7 +130,88 @@
             o_ref[pl.ds(f * 2 * MEMBERS + r, MEMBERS, stride=2), :] = post + c_ref[k:k+1, :]
 
 
-def assimilate(turn_ref, state_ref, west_ref, east_ref, south_ref, north_ref, weight_ref, sent_ref, anomaly_ref, center_ref, wide):
+def turned(even_ref, prior_ref, state_ref, edge_ref, rows_ref):
+    cols = MEMBERS
+    even = even_ref[0:1, :] > 0.5
+    for f in range(3):
+        rows_ref[...] = prior_ref[2 * cols * f:2 * cols * (f + 1), :].astype(jnp.float32)
+        for r in range(2):
+            k = 2 * f + r
+            block = rows_ref[pl.ds(r, cols, stride=2), :].T
+            state_ref[k * cols:(k + 1) * cols, :] = block
+            edge_ref[2 * k:2 * k + 2, :] = jnp.where(even, block[:2, :], block[cols - 2:, :])
+
+
+def inner_edges(even_ref, state_ref, after_ref, edge_ref):
+    cols = MEMBERS
+    even = even_ref[0:1, :] > 0.5
+    for k in range(6):
+        low, high = state_ref[k * cols:k * cols + 2, :], state_ref[(k + 1) * cols - 2:(k + 1) * cols, :]
+        edge_ref[2 * k:2 * k + 2, :] = jnp.where(even, high, low)
+
+
+def row_of(state_ref, f, first):
+    cols = MEMBERS
+    low = state_ref[2 * f * cols:(2 * f + 1) * cols, :]
+    high = state_ref[(2 * f + 1) * cols:(2 * f + 2) * cols, :]
+    return jnp.where(first, low, high)
+
+
+def early_rows(turn_ref, state_ref, out_ref):
+    cols = MEMBERS
+    first = turn_ref[6:7, :] < 0.5
+    step = (2.0 * HALF_COURANT) * turn_ref[6:7, :] - HALF_COURANT
+    spin = jnp.where(first, turn_ref[1:2, :], turn_ref[2:3, :])
+    h, u, v = (row_of(state_ref, f, first) for f in range(3))
+    out_ref[:cols, :] = h
+    out_ref[cols:2 * cols, :] = v
+    out_ref[2 * cols:, :] = v + step * row_of(state_ref, 0, ~first) - spin * u
+
+
+def edge_rows(state_ref, west_ref, east_ref, wide, first, step):
+    cols = MEMBERS
+
+    def beside(ref, f, c):
+        k = 4 * f + c
+        return jnp.where(first, ref[k:k + 1, :], ref[k + 2:k + 3, :])
+
+    wide[8:8 + cols, :] = row_of(state_ref, 1, first)
+    wide[7:8, :] = beside(west_ref, 1, 1)
+    wide[8 + cols:9 + cols, :] = beside(east_ref, 1, 0)
+    slope = wide[9:9 + cols, :] - wide[7:7 + cols, :]
+    mid = row_of(state_ref, 0, first) - HALF_COURANT * slope + step * row_of(state_ref, 2, ~first)
+    return mid, beside(west_ref, 2, 1), beside(east_ref, 2, 0)
+
+
+def late_rows(turn_ref, state_ref, west_ref, east_ref, out_ref, wide):
+    cols = MEMBERS
+    first = turn_ref[6:7, :] < 0.5
+    step = (2.0 * HALF_COURANT) * turn_ref[6:7, :] - HALF_COURANT
+    mid, west_v, east_v = edge_rows(state_ref, west_ref, east_ref, wide, first, step)
+    out_ref[:cols, :] = mid
+    out_ref[cols:cols + 1, :] = west_v
+    out_ref[cols + 1:cols + 2, :] = east_v
+
+
+def inner_rows(turn_ref, state_ref, west_ref, east_ref, after_ref, out_ref, wide):
+    cols = MEMBERS
+    first = turn_ref[6:7, :] > 0.5
+    step = HALF_COURANT - (2.0 * HALF_COURANT) * turn_ref[6:7, :]
+    spin = jnp.where(first, turn_ref[1:2, :], turn_ref[2:3, :])
+    mid, west_v, east_v = edge_rows(state_ref, west_ref, east_ref, wide, first, step)
+    h, u, v = (row_of(state_ref, f, first) for f in range(3))
+    out_ref[:cols, :] = h
+    out_ref[cols:2 * cols, :] = v
+    out_ref[2 * cols:3 * cols, :] = v + step * row_of(state_ref, 0, ~first) - spin * u
+    out_ref[3 * cols:4 * cols, :] = mid
+    out_ref[4 * cols:4 * cols + 1, :] = west_v
+    out_ref[4 * cols + 1:4 * cols + 2, :] = east_v
+
+
+def assimilate(
+    turn_ref, state_ref, west_ref, east_ref, early_ref, late_ref, inner_ref, weight_ref,
+    sent_ref, anomaly_ref, center_ref, wide,
+):
     a = HALF_COURANT
     cols = MEMBERS
 
@@ -157,17 +231,24 @@
     def slope(slot):
         return wide[slot, 9:9 + cols, :] - wide[slot, 7:7 + cols, :]
 
-    spin = [turn_ref[1], turn_ref[2]]
+    spin = [turn_ref[1:2, :], turn_ref[2:3, :]]
     h = [field(0, 0), field(0, 1)]
     u = [field(1, 0), field(1, 1)]
     v = [field(2, 0), field(2, 1)]
     for r in range(2):
         place(4 + r, h[r], beside(west_ref, 0, r, 1), beside(east_ref, 0, r, 0))
         place(6 + r, u[r], beside(west_ref, 1, r, 1), beside(east_ref, 1, r, 0))
-    south_h, south_v, south_mid_v, south_mid_h = (south_ref[k * cols:(k + 1) * cols, :] for k in range(4))
-    north_h, north_v, north_mid_v, north_mid_h = (north_ref[k * cols:(k + 1) * cols, :] for k in range(4))
-    south_edge = [south_ref[4 * cols + k:4 * cols + k + 1, :] for k in range(2)]
-    north_edge = [north_ref[4 * cols + k:4 * cols + k + 1, :] for k in range(2)]
+    even = turn_ref[6:7, :] < 0.5
+    outer = [early_ref[k * cols:(k + 1) * cols, :] for k in range(3)] + [late_ref[:cols, :]]
+    inner = [inner_ref[k * cols:(k + 1) * cols, :] for k in range(4)]
+    outer += [late_ref[cols + k:cols + k + 1, :] for k in range(2)]
+    inner += [inner_ref[4 * cols + k:4 * cols + k + 1, :] for k in range(2)]
+    south_h, south_v, south_mid_v, south_mid_h, *south_edge = (
+        jnp.where(even, o, i) for o, i in zip(outer, inner)
+    )
+    north_h, north_v, north_mid_v, north_mid_h, *north_edge = (
+        jnp.where(even, i, o) for o, i in zip(outer, inner)
+    )
     h_below, h_above = [south_h, h[0]], [h[1], north_h]
     v_below, v_above = [south_v, v[0]], [v[1], north_v]
     rate_h, rate_u, rate_v, mid_h, mid_u, mid_v = [], [], [], [], [], []
@@ -196,7 +277,7 @@
             )
         place(r, mid_h[r], *outside_h)
         place(2 + r, mid_u[r], *outside_u)
-    has_south, has_north = turn_ref[4], turn_ref[5]
+    has_south, has_north = turn_ref[4:5, :], turn_ref[5:6, :]
     south_mid_h = has_south * (south_mid_h - a * v[0])
     south_mid_v = has_south * (south_mid_v - a * h[0])
     north_mid_h = has_north * (north_mid_h + a * v[1])
@@ -250,33 +331,56 @@
     has_south = (lat_index > 0).astype(jnp.float32)
     has_north = (lat_index < lat_count - 1).astype(jnp.float32)
 
-    state = jnp.transpose(prior_ensemble, (0, 2, 3, 1)).astype(jnp.float32)
-    west, east = swap(state[:, :, :2], state[:, :, -2:], lon_even, LON, lon_perms)
+    vmem = pl.BlockSpec(memory_space=pltpu.VMEM)
+    params = pltpu.CompilerParams(vmem_limit_bytes=16 * 1024 * 1024)
+    small = pl.CostEstimate(flops=10**5, bytes_accessed=10**5, transcendentals=0)
+    edges = 2 * 3 * rows
+
+    def shaped(*heights):
+        return [jax.ShapeDtypeStruct((height, members), jnp.float32) for height in heights]
+
+    lon_flag = jnp.broadcast_to(lon_even.astype(jnp.float32), (8, members))
+    state, outer_edge = pl.pallas_call(
+        turned,
+        in_specs=[vmem] * 2,
+        out_specs=[vmem] * 2,
+        out_shape=shaped(entries, edges),
+        scratch_shapes=[pltpu.VMEM((rows * members, cols), jnp.float32)],
+        compiler_params=params,
+        cost_estimate=small,
+    )(lon_flag, prior_ensemble.reshape(entries, cols))
+    lon_inner, lon_outer = lon_perms
+    outer_edge = lax.ppermute(outer_edge, LON, lon_outer)
 
     inner_perm, outer_perm = lat_perms
-    h, u, v = state[0], state[1], state[2]
-
-    def early(row, other, sign, spin):
-        return jnp.concatenate([h[row], v[row], v[row] + sign * a * h[other] - spin * u[row]])
-
-    down_early, up_early = early(0, 1, -1.0, turn[1]), early(1, 0, 1.0, turn[2])
-    outer_early = lax.ppermute(jnp.where(lat_even, down_early, up_early), LAT, outer_perm)
-
-    def late(row, other, sign):
-        around = jnp.concatenate([west[1, row, 1:], u[row], east[1, row, :1]])
-        mid = h[row] - a * (around[2:] - around[:-2]) + sign * a * v[other]
-        return jnp.concatenate([mid, west[2, row, 1:], east[2, row, :1]])
-
-    down_late, up_late = late(0, 1, -1.0), late(1, 0, 1.0)
-    outer_late = lax.ppermute(jnp.where(lat_even, down_late, up_late), LAT, outer_perm)
-    inner = lax.ppermute(
-        jnp.where(
-            lat_even, jnp.concatenate([up_early, up_late]), jnp.concatenate([down_early, down_late])
-        ),
-        LAT, inner_perm,
-    )
-    outer = jnp.concatenate([outer_early, outer_late])
-    south, north = jnp.where(lat_even, outer, inner), jnp.where(lat_even, inner, outer)
+    edge_row = 1.0 - lat_even.astype(jnp.float32)
+    scalars = jnp.concatenate([turn, jnp.stack([has_south, has_north, edge_row, edge_row])])
+    scalars = jnp.broadcast_to(scalars[:, None], (8, members))
+    early = pl.pallas_call(
+        early_rows, in_specs=[vmem] * 2, out_specs=vmem, out_shape=shaped(3 * cols)[0],
+        compiler_params=params, cost_estimate=small,
+    )(scalars, state)
+    outer_early = lax.ppermute(early, LAT, outer_perm)
+
+    inner_edge = pl.pallas_call(
+        inner_edges, in_specs=[vmem] * 3, out_specs=vmem, out_shape=shaped(edges)[0],
+        compiler_params=params, cost_estimate=small,
+    )(lon_flag, state, early)
+    inner_edge = lax.ppermute(inner_edge, LON, lon_inner)
+    west = jnp.where(lon_even, outer_edge, inner_edge)
+    east = jnp.where(lon_even, inner_edge, outer_edge)
+
+    wide_row = [pltpu.VMEM((cols + 16, members), jnp.float32)]
+    late = pl.pallas_call(
+        late_rows, in_specs=[vmem] * 4, out_specs=vmem, out_shape=shaped(cols + 2)[0],
+        scratch_shapes=wide_row, compiler_params=params, cost_estimate=small,
+    )(scalars, state, west, east)
+    outer_late = lax.ppermute(late, LAT, outer_perm)
+    inner = pl.pallas_call(
+        inner_rows, in_specs=[vmem] * 5, out_specs=vmem, out_shape=shaped(4 * cols + 2)[0],
+        scratch_shapes=wide_row, compiler_params=params, cost_estimate=small,
+    )(scalars, state, west, east, late)
+    inner = lax.ppermute(inner, LAT, inner_perm)
 
     index = obs_index.reshape(-1)
     slots = index.shape[0]
@@ -287,11 +391,9 @@
     weights = jnp.dot(
         named, jnp.stack([weight, weight * observed.reshape(-1)], axis=1), precision=lax.Precision.HIGHEST
     )
-    scalars = jnp.concatenate([turn, jnp.stack([has_south, has_north])])
-    vmem = pl.BlockSpec(memory_space=pltpu.VMEM)
     sent, anomaly, center = pl.pallas_call(
         assimilate,
-        in_specs=[pl.BlockSpec(memory_space=pltpu.SMEM)] + [vmem] * 6,
+        in_specs=[vmem] * 8,
         out_specs=[vmem] * 3,
         out_shape=[
             jax.ShapeDtypeStruct((members, members), jnp.float32),
@@ -299,18 +401,17 @@
             jax.ShapeDtypeStruct((3 * rows, cols), jnp.float32),
         ],
         scratch_shapes=[pltpu.VMEM((8, cols + 16, members), jnp.float32)],
-        compiler_params=pltpu.CompilerParams(vmem_limit_bytes=16 * 1024 * 1024),
+        compiler_params=params,
         cost_estimate=pl.CostEstimate(flops=3 * 10**7, bytes_accessed=2 * 10**6, transcendentals=0),
     )(
-        scalars, state.reshape(entries, members), west.reshape(-1, members), east.reshape(-1, members),
-        south, north, weights,
+        scalars, state, west, east, outer_early, outer_late, inner, weights,
     )
     total = all_sum(sent)
     posterior = pl.pallas_call(
         finish,
         out_shape=jax.ShapeDtypeStruct((entries, cols), jnp.float32),
         scratch_shapes=[pltpu.VMEM((members, 2 * members), jnp.float32)],
-        compiler_params=pltpu.CompilerParams(vmem_limit_bytes=16 * 1024 * 1024),
+        compiler_params=params,
         cost_estimate=pl.CostEstimate(flops=3 * 10**7, bytes_accessed=10**6, transcendentals=0),
     )(total, anomaly, center)
     return posterior.reshape(3, members, rows, cols)

time: 110 us -> 105 us (0.955)
  waiting for transfers between devices: 8.06 us -> 5.92 us
  other arithmetic: 1.77 us -> 0.14 us
  local copies, waits for them, and re-layouts: 3.23 us -> 1.79 us
    ppermute x5, waiting for transfers between devices: 8.06 us -> 5.92 us  [the longest x1 5.91 us: shards(): outer_late = lax.ppermute(late, LAT, outer_perm)]
  transfers between devices with their start and end apart: 5 -> 5, of which waited for: 2 -> 1; matrix products, arithmetic and copies ran while one was open for 2% -> 0% of each run, Pallas kernels for 0% -> 0%
where the time goes in v5:
time: 105 us
  blocking collectives  51.7 us (49%)
  starting transfers between devices  36.1 us (34%)
  Pallas kernels  7.58 us (7%)
  waiting for transfers between devices  5.92 us (6%)
  local copies, waits for them, and re-layouts  1.79 us (2%)
    all_to_all x1, blocking collectives, all_sum(): lax.all_to_all(block.reshape(plane, part, cols), PLANE, 0, 0, tiled=True)  22 us
    all_to_all x1, blocking collectives, all_sum(): lax.all_to_all(jnp.broadcast_to(mine[None], (line, part, cols)), LINE, 0,...  17.3 us
    ppermute x1, starting transfers between devices, shards(): outer_edge = lax.ppermute(outer_edge, LON, lon_outer)  16.2 us
    all_to_all x1, blocking collectives, all_sum(): lax.all_to_all(jnp.broadcast_to(mine[None], (plane, part, cols)), PLANE,...  12.3 us
    ppermute x1, starting transfers between devices, shards(): outer_early = lax.ppermute(early, LAT, outer_perm)  8.78 us
    ppermute x1, starting transfers between devices, shards(): outer_late = lax.ppermute(late, LAT, outer_perm)  7.37 us
    ppermute x1, waiting for transfers between devices, shards(): outer_late = lax.ppermute(late, LAT, outer_perm)  5.91 us
    pallas_call x1, Pallas kernels, shards(): pl.pallas_call(finish, out_shape=jax.ShapeDtypeStruct((entries, cols), jn...  5.91 us
  transfers between devices with their start and end apart: 5, of which 1 were waited for; matrix products, arithmetic and copies ran while one was open for 0% of the time, Pallas kernels for 0%

profile of v5, /device:TPU:1, one launch (start us, length us, event | category | flops | bytes accessed | tf_op | source)
XLA Modules:
  0.0 104.6 jit_solution(5389539319110071408)
XLA Ops:
  0.1 0.0 copy-start
  0.1 0.9 copy-done
  1.0 0.1 shard_map.55
  1.1 0.1 concatenate.3
  1.2 0.1 broadcast_in_dim.8.turn_ref
  1.3 16.2 %collective-permute-start = (f32[12,128]{1,0:T(8,128)S(1)}, f32[12,128]{1,0:T(8,128)S(1)}, u32[]{:S(2)}, u32[]{:S(2)}) collective-permute-start(f32[12,128]{1,0:T(8,128)S(1)} %get-tuple-element.11), channel_id=1, source_target_pairs={{1,2},{2,1},{3,4},{4,3},{5,6},{6,5},{7,8},{8,7},{9,10},{10,9},{11,... | collective-permute-start | bytes 18440 | tf_op jit(solution)/shard_map/ppermute | solution.py:353
  17.5 1.9 %collective-permute-start.1 = (f32[12,128]{1,0:T(8,128)S(1)}, f32[12,128]{1,0:T(8,128)S(1)}, u32[]{:S(2)}, u32[]{:S(2)}) collective-permute-start(f32[12,128]{1,0:T(8,128)S(1)} %shard_map.57), channel_id=1, source_target_pairs={{0,1},{1,0},{2,3},{3,2},{4,5},{5,4},{6,7},{7,6},{8,9},{9,8},{10,11... | collective-permute-start | bytes 18440 | tf_op jit(solution)/shard_map/ppermute | solution.py:369
  19.5 8.8 %collective-permute-start.2 = (f32[384,128]{1,0:T(8,128)S(1)}, f32[384,128]{1,0:T(8,128)S(1)}, u32[]{:S(2)}, u32[]{:S(2)}) collective-permute-start(f32[384,128]{1,0:T(8,128)S(1)} %shard_map.56.after_ref), channel_id=1, source_target_pairs={{32,64},{64,32},{96,128},{128,96},{160,192},{192,160},{224,256},{2... | collective-permute-start | bytes 589832 | tf_op jit(solution)/shard_map/ppermute | solution.py:363
  28.2 0.0 collective-permute-done
  28.3 0.0 collective-permute-done.1
  29.0 0.0 copy-start.3
  29.0 0.1 shard_map.59
  29.0 0.0 copy-start.2
  29.1 1.9 %collective-permute-start.4 = (f32[514,128]{1,0:T(8,128)S(1)}, f32[514,128]{1,0:T(8,128)S(1)}, u32[]{:S(2)}, u32[]{:S(2)}) collective-permute-start(f32[514,128]{1,0:T(8,128)S(1)} %shard_map.59), channel_id=1, source_target_pairs={{0,32},{32,0},{64,96},{96,64},{128,160},{160,128},{192,224},{224,1... | collective-permute-start | bytes 789512 | tf_op jit(solution)/shard_map/ppermute | solution.py:383
  31.0 0.0 copy-done.3
  31.0 0.0 copy-done.2
  31.0 7.4 %collective-permute-start.3 = (f32[130,128]{1,0:T(8,128)S(1)}, f32[130,128]{1,0:T(8,128)S(1)}, u32[]{:S(2)}, u32[]{:S(2)}) collective-permute-start(f32[130,128]{1,0:T(8,128)S(1)} %shard_map.58.after_ref), channel_id=1, source_target_pairs={{32,64},{64,32},{96,128},{128,96},{160,192},{192,160},{224,256},{2... | collective-permute-start | bytes 199688 | tf_op jit(solution)/shard_map/ppermute | solution.py:378
  38.4 0.0 copy-start.1
  38.4 0.7 copy-done.1
  39.1 0.5 fusion.weight_ref
  39.5 5.9 %collective-permute-done.3.late_ref = f32[130,128]{1,0:T(8,128)S(1)} collective-permute-done((f32[130,128]{1,0:T(8,128)S(1)}, f32[130,128]{1,0:T(8,128)S(1)}, u32[]{:S(2)}, u32[]{:S(2)}) %collective-permute-start.3) | collective-permute-done | bytes 66592 | tf_op jit(solution)/shard_map/ppermute | solution.py:378
  45.5 0.0 collective-permute-done.2.early_ref
  45.5 0.0 collective-permute-done.4.inner_ref
  45.5 1.4 %shard_map.60 = (f32[128,128]{1,0:T(8,128)S(1)}, f32[768,128]{1,0:T(8,128)S(1)}, f32[6,128]{1,0:T(8,128)S(1)}) custom-call(f32[8,128]{1,0:T(8,128)S(1)} %broadcast_in_dim.8.turn_ref, f32[768,128]{1,0:T(8,128)S(1)} %get-tuple-element.10.state_ref, f32[12,128]{1,0:T(8,128)S(1)} %get-tuple-element.18.west_ref, f32[12,128]{1,0:T(8,128)S(1)} %get-tuple-element.17.east_ref, ...), custom_call_target="tpu_custom_call" | custom-call | flops 30000000 | bytes 2000000 | tf_op jit(solution)/shard_map/pallas_call | solution.py:394
  46.9 22.0 %all_to_all.15 = f32[32,4,128]{2,1,0:T(4,128)S(1)} all-to-all(f32[32,4,128]{2,1,0:T(4,128)S(1)} %bitcast.17), channel_id=1, replica_groups=mesh['x'=4,'zh'=2,'core'=2,'zl'=8,'y'=4] {'x','core','y'}, dimensions={0} | all-to-all | bytes 131072 | tf_op jit(solution)/shard_map/all_to_all | solution.py:41
  68.9 17.3 %all_to_all.16 = f32[16,4,128]{2,1,0:T(4,128)S(1)} all-to-all(f32[16,4,128]{2,1,0:T(4,128)S(1)} %broadcast_in_dim.10), channel_id=1, replica_groups=mesh['x'=4,'zh'=2,'core'=2,'zl'=8,'y'=4] {'zh','zl'}, dimensions={0} | all-to-all | bytes 65536 | tf_op jit(solution)/shard_map/all_to_all | solution.py:42
  86.3 12.3 %all_to_all.17 = f32[32,4,128]{2,1,0:T(4,128)S(1)} all-to-all(f32[32,4,128]{2,1,0:T(4,128)S(1)} %broadcast_in_dim.11), channel_id=1, replica_groups=mesh['x'=4,'zh'=2,'core'=2,'zl'=8,'y'=4] {'x','core','y'}, dimensions={0} | all-to-all | bytes 131072 | tf_op jit(solution)/shard_map/all_to_all | solution.py:45
  98.7 5.9 %shard_map.61 = f32[768,128]{1,0:T(8,128)} custom-call(f32[128,128]{1,0:T(8,128)S(1)} %bitcast.15, f32[768,128]{1,0:T(8,128)S(1)} %get-tuple-element.13.x_ref, f32[6,128]{1,0:T(8,128)S(1)} %get-tuple-element.14.c_ref), custom_call_target="tpu_custom_call" | custom-call | flops 30000000 | bytes 1000000 | tf_op jit(solution)/shard_map/pallas_call | solution.py:410
  (11 shorter events, 0.2 us)
Async XLA Ops:
  0.1 0.9 copy-start
  1.3 26.9 %collective-permute-start = (f32[12,128]{1,0:T(8,128)S(1)}, f32[12,128]{1,0:T(8,128)S(1)}, u32[]{:S(2)}, u32[]{:S(2)}) collective-permute-start(f32[12,128]{1,0:T(8,128)S(1)} %get-tuple-element.11), channel_id=1, source_target_pairs={{1,2},{2,1},{3,4},{4,3},{5,6},{6,5},{7,8},{8,7},{9,10},{10,9},{11,... | collective-permute-start | bytes 18440 | tf_op jit(solution)/shard_map/ppermute | solution.py:353
  17.5 10.7 %collective-permute-start.1 = (f32[12,128]{1,0:T(8,128)S(1)}, f32[12,128]{1,0:T(8,128)S(1)}, u32[]{:S(2)}, u32[]{:S(2)}) collective-permute-start(f32[12,128]{1,0:T(8,128)S(1)} %shard_map.57), channel_id=1, source_target_pairs={{0,1},{1,0},{2,3},{3,2},{4,5},{5,4},{6,7},{7,6},{8,9},{9,8},{10,11... | collective-permute-start | bytes 18440 | tf_op jit(solution)/shard_map/ppermute | solution.py:369
  19.5 26.0 %collective-permute-start.2 = (f32[384,128]{1,0:T(8,128)S(1)}, f32[384,128]{1,0:T(8,128)S(1)}, u32[]{:S(2)}, u32[]{:S(2)}) collective-permute-start(f32[384,128]{1,0:T(8,128)S(1)} %shard_map.56.after_ref), channel_id=1, source_target_pairs={{32,64},{64,32},{96,128},{128,96},{160,192},{192,160},{224,256},{2... | collective-permute-start | bytes 589832 | tf_op jit(solution)/shard_map/ppermute | solution.py:363
  29.0 2.0 %copy-start.3 = (f32[1,1,256]{2,1,0:T(1,128)S(1)}, f32[1,1,256]{2,1,0:T(1,128)}, u32[]{:S(2)}) copy-start(f32[1,1,256]{2,1,0:T(1,128)} %param.7) | copy-start | bytes 3076
  29.0 2.0 %copy-start.2 = (f32[1,1,256]{2,1,0:T(1,128)S(1)}, f32[1,1,256]{2,1,0:T(1,128)}, u32[]{:S(2)}) copy-start(f32[1,1,256]{2,1,0:T(1,128)} %param.6) | copy-start | bytes 3076
  29.1 16.4 %collective-permute-start.4 = (f32[514,128]{1,0:T(8,128)S(1)}, f32[514,128]{1,0:T(8,128)S(1)}, u32[]{:S(2)}, u32[]{:S(2)}) collective-permute-start(f32[514,128]{1,0:T(8,128)S(1)} %shard_map.59), channel_id=1, source_target_pairs={{0,32},{32,0},{64,96},{96,64},{128,160},{160,128},{192,224},{224,1... | collective-permute-start | bytes 789512 | tf_op jit(solution)/shard_map/ppermute | solution.py:383
  31.0 14.4 %collective-permute-start.3 = (f32[130,128]{1,0:T(8,128)S(1)}, f32[130,128]{1,0:T(8,128)S(1)}, u32[]{:S(2)}, u32[]{:S(2)}) collective-permute-start(f32[130,128]{1,0:T(8,128)S(1)} %shard_map.58.after_ref), channel_id=1, source_target_pairs={{32,64},{64,32},{96,128},{128,96},{160,192},{192,160},{224,256},{2... | collective-permute-start | bytes 199688 | tf_op jit(solution)/shard_map/ppermute | solution.py:378
  38.4 0.7 copy-start.1

commit v6 on v5

--- a/solution.py
+++ b/solution.py
@@ -124,10 +124,13 @@
     mean_weights = jnp.dot(forward, inverse, precision=lax.Precision.HIGHEST, preferred_element_type=jnp.float32)
     weights = math.sqrt(prior) * inverse + mean_weights[0:1, :]
     for f in range(3):
+        post = lax.dot_general(
+            weights, x_ref[2 * f * MEMBERS:2 * (f + 1) * MEMBERS, :], (((1,), (1,)), ((), ())),
+            precision=lax.Precision.HIGHEST, preferred_element_type=jnp.float32,
+        )
         for r in range(2):
-            k = 2 * f + r
-            post = lax.dot_general(weights, x_ref[k * MEMBERS:(k + 1) * MEMBERS, :], (((1,), (1,)), ((), ())), precision=lax.Precision.HIGHEST, preferred_element_type=jnp.float32)
-            o_ref[pl.ds(f * 2 * MEMBERS + r, MEMBERS, stride=2), :] = post + c_ref[k:k+1, :]
+            center = c_ref[2 * f + r:2 * f + r + 1, :]
+            o_ref[pl.ds(2 * f * MEMBERS + r, MEMBERS, stride=2), :] = post[:, r * MEMBERS:(r + 1) * MEMBERS] + center
 
 
 def turned(even_ref, prior_ref, state_ref, edge_ref, rows_ref):
@@ -294,7 +297,7 @@
         forecast[4 + r] = v[r] + 0.5 * (rate_v[r] + second_v)
     share = jnp.full((8, MEMBERS), 1.0 / MEMBERS, jnp.float32)
     push = jnp.zeros((1, MEMBERS), jnp.float32)
-    gram = jnp.zeros((MEMBERS, MEMBERS), jnp.float32)
+    anomalies, weighted = [], []
     for k in range(6):
         mean = jnp.sum(forecast[k], axis=1, keepdims=True) * (1.0 / MEMBERS)
         anomaly = forecast[k] - mean
@@ -307,10 +310,12 @@
         weight = weight_ref[k * cols:(k + 1) * cols, 0:1]
         pull = weight_ref[k * cols:(k + 1) * cols, 1:2] - weight * mean
         push = push + jnp.sum(pull * anomaly, axis=0, keepdims=True)
-        gram = gram + lax.dot_general(
-            weight * anomaly, anomaly, (((0,), (0,)), ((), ())), precision=lax.Precision.HIGHEST,
-            preferred_element_type=jnp.float32,
-        )
+        anomalies.append(anomaly)
+        weighted.append(weight * anomaly)
+    gram = lax.dot_general(
+        jnp.concatenate(weighted, axis=0), jnp.concatenate(anomalies, axis=0), (((0,), (0,)), ((), ())),
+        precision=lax.Precision.HIGHEST, preferred_element_type=jnp.float32,
+    )
     row_at = lax.broadcasted_iota(jnp.int32, (MEMBERS, MEMBERS), 0)
     col_at = lax.broadcasted_iota(jnp.int32, (MEMBERS, MEMBERS), 1)
     sent = jnp.where((row_at == MEMBERS - 1) & (col_at < MEMBERS - 1), push, gram)

time: 105 us -> 105 us (level)
  no operation moved by 1% of the time
where the time goes in v6:
time: 105 us; the launch traced here: 104 us
  blocking collectives  51.7 us (49%)
  starting transfers between devices  36.1 us (34%)
  Pallas kernels  7.23 us (7%)
  waiting for transfers between devices  5.92 us (6%)
  local copies, waits for them, and re-layouts  1.79 us (2%)
    all_to_all x1, blocking collectives, all_sum(): lax.all_to_all(block.reshape(plane, part, cols), PLANE, 0, 0, tiled=True)  22 us
    all_to_all x1, blocking collectives, all_sum(): lax.all_to_all(jnp.broadcast_to(mine[None], (line, part, cols)), LINE, 0,...  17.3 us
    ppermute x1, starting transfers between devices, shards(): outer_edge = lax.ppermute(outer_edge, LON, lon_outer)  16.2 us
    all_to_all x1, blocking collectives, all_sum(): lax.all_to_all(jnp.broadcast_to(mine[None], (plane, part, cols)), PLANE,...  12.3 us
    ppermute x1, starting transfers between devices, shards(): outer_early = lax.ppermute(early, LAT, outer_perm)  8.78 us
    ppermute x1, starting transfers between devices, shards(): outer_late = lax.ppermute(late, LAT, outer_perm)  7.37 us
    ppermute x1, waiting for transfers between devices, shards(): outer_late = lax.ppermute(late, LAT, outer_perm)  5.91 us
    pallas_call x1, Pallas kernels, shards(): pl.pallas_call(finish, out_shape=jax.ShapeDtypeStruct((entries, cols), jn...  5.64 us
  transfers between devices with their start and end apart: 5, of which 1 were waited for; matrix products, arithmetic and copies ran while one was open for 0% of the time, Pallas kernels for 0%

profile of v6, /device:TPU:1, one launch (start us, length us, event | category | flops | bytes accessed | tf_op | source)
XLA Modules:
  0.0 104.2 jit_solution(16521997885714981284)
XLA Ops:
  0.1 0.0 copy-start
  0.1 0.9 copy-done
  1.0 0.1 shard_map.55
  1.1 0.1 concatenate.3
  1.2 0.1 broadcast_in_dim.8.turn_ref
  1.3 16.2 %collective-permute-start = (f32[12,128]{1,0:T(8,128)S(1)}, f32[12,128]{1,0:T(8,128)S(1)}, u32[]{:S(2)}, u32[]{:S(2)}) collective-permute-start(f32[12,128]{1,0:T(8,128)S(1)} %get-tuple-element.11), channel_id=1, source_target_pairs={{1,2},{2,1},{3,4},{4,3},{5,6},{6,5},{7,8},{8,7},{9,10},{10,9},{11,... | collective-permute-start | bytes 18440 | tf_op jit(solution)/shard_map/ppermute | solution.py:358
  17.5 1.9 %collective-permute-start.1 = (f32[12,128]{1,0:T(8,128)S(1)}, f32[12,128]{1,0:T(8,128)S(1)}, u32[]{:S(2)}, u32[]{:S(2)}) collective-permute-start(f32[12,128]{1,0:T(8,128)S(1)} %shard_map.57), channel_id=1, source_target_pairs={{0,1},{1,0},{2,3},{3,2},{4,5},{5,4},{6,7},{7,6},{8,9},{9,8},{10,11... | collective-permute-start | bytes 18440 | tf_op jit(solution)/shard_map/ppermute | solution.py:374
  19.5 8.8 %collective-permute-start.2 = (f32[384,128]{1,0:T(8,128)S(1)}, f32[384,128]{1,0:T(8,128)S(1)}, u32[]{:S(2)}, u32[]{:S(2)}) collective-permute-start(f32[384,128]{1,0:T(8,128)S(1)} %shard_map.56.after_ref), channel_id=1, source_target_pairs={{32,64},{64,32},{96,128},{128,96},{160,192},{192,160},{224,256},{2... | collective-permute-start | bytes 589832 | tf_op jit(solution)/shard_map/ppermute | solution.py:368
  28.2 0.0 collective-permute-done
  28.3 0.0 collective-permute-done.1
  29.0 0.0 copy-start.3
  29.0 0.1 shard_map.59
  29.0 0.0 copy-start.2
  29.1 1.9 %collective-permute-start.4 = (f32[514,128]{1,0:T(8,128)S(1)}, f32[514,128]{1,0:T(8,128)S(1)}, u32[]{:S(2)}, u32[]{:S(2)}) collective-permute-start(f32[514,128]{1,0:T(8,128)S(1)} %shard_map.59), channel_id=1, source_target_pairs={{0,32},{32,0},{64,96},{96,64},{128,160},{160,128},{192,224},{224,1... | collective-permute-start | bytes 789512 | tf_op jit(solution)/shard_map/ppermute | solution.py:388
  31.0 0.0 copy-done.3
  31.0 0.0 copy-done.2
  31.0 7.4 %collective-permute-start.3 = (f32[130,128]{1,0:T(8,128)S(1)}, f32[130,128]{1,0:T(8,128)S(1)}, u32[]{:S(2)}, u32[]{:S(2)}) collective-permute-start(f32[130,128]{1,0:T(8,128)S(1)} %shard_map.58.after_ref), channel_id=1, source_target_pairs={{32,64},{64,32},{96,128},{128,96},{160,192},{192,160},{224,256},{2... | collective-permute-start | bytes 199688 | tf_op jit(solution)/shard_map/ppermute | solution.py:383
  38.4 0.0 copy-start.1
  38.4 0.7 copy-done.1
  39.1 0.5 fusion.weight_ref
  39.5 5.9 %collective-permute-done.3.late_ref = f32[130,128]{1,0:T(8,128)S(1)} collective-permute-done((f32[130,128]{1,0:T(8,128)S(1)}, f32[130,128]{1,0:T(8,128)S(1)}, u32[]{:S(2)}, u32[]{:S(2)}) %collective-permute-start.3) | collective-permute-done | bytes 66592 | tf_op jit(solution)/shard_map/ppermute | solution.py:383
  45.5 0.0 collective-permute-done.2.early_ref
  45.5 0.0 collective-permute-done.4.inner_ref
  45.5 1.3 %shard_map.60 = (f32[128,128]{1,0:T(8,128)S(1)}, f32[768,128]{1,0:T(8,128)S(1)}, f32[6,128]{1,0:T(8,128)S(1)}) custom-call(f32[8,128]{1,0:T(8,128)S(1)} %broadcast_in_dim.8.turn_ref, f32[768,128]{1,0:T(8,128)S(1)} %get-tuple-element.10.state_ref, f32[12,128]{1,0:T(8,128)S(1)} %get-tuple-element.18.west_ref, f32[12,128]{1,0:T(8,128)S(1)} %get-tuple-element.17.east_ref, ...), custom_call_target="tpu_custom_call" | custom-call | flops 30000000 | bytes 2000000 | tf_op jit(solution)/shard_map/pallas_call | solution.py:399
  46.8 22.0 %all_to_all.15 = f32[32,4,128]{2,1,0:T(4,128)S(1)} all-to-all(f32[32,4,128]{2,1,0:T(4,128)S(1)} %bitcast.17), channel_id=1, replica_groups=mesh['x'=4,'zh'=2,'core'=2,'zl'=8,'y'=4] {'x','core','y'}, dimensions={0} | all-to-all | bytes 131072 | tf_op jit(solution)/shard_map/all_to_all | solution.py:41
  68.8 17.3 %all_to_all.16 = f32[16,4,128]{2,1,0:T(4,128)S(1)} all-to-all(f32[16,4,128]{2,1,0:T(4,128)S(1)} %broadcast_in_dim.10), channel_id=1, replica_groups=mesh['x'=4,'zh'=2,'core'=2,'zl'=8,'y'=4] {'zh','zl'}, dimensions={0} | all-to-all | bytes 65536 | tf_op jit(solution)/shard_map/all_to_all | solution.py:42
  86.2 12.3 %all_to_all.17 = f32[32,4,128]{2,1,0:T(4,128)S(1)} all-to-all(f32[32,4,128]{2,1,0:T(4,128)S(1)} %broadcast_in_dim.11), channel_id=1, replica_groups=mesh['x'=4,'zh'=2,'core'=2,'zl'=8,'y'=4] {'x','core','y'}, dimensions={0} | all-to-all | bytes 131072 | tf_op jit(solution)/shard_map/all_to_all | solution.py:45
  98.6 5.6 %shard_map.61 = f32[768,128]{1,0:T(8,128)} custom-call(f32[128,128]{1,0:T(8,128)S(1)} %bitcast.15, f32[768,128]{1,0:T(8,128)S(1)} %get-tuple-element.13.x_ref, f32[6,128]{1,0:T(8,128)S(1)} %get-tuple-element.14.c_ref), custom_call_target="tpu_custom_call" | custom-call | flops 30000000 | bytes 1000000 | tf_op jit(solution)/shard_map/pallas_call | solution.py:415
  (11 shorter events, 0.2 us)
Async XLA Ops:
  0.1 0.9 copy-start
  1.3 26.9 %collective-permute-start = (f32[12,128]{1,0:T(8,128)S(1)}, f32[12,128]{1,0:T(8,128)S(1)}, u32[]{:S(2)}, u32[]{:S(2)}) collective-permute-start(f32[12,128]{1,0:T(8,128)S(1)} %get-tuple-element.11), channel_id=1, source_target_pairs={{1,2},{2,1},{3,4},{4,3},{5,6},{6,5},{7,8},{8,7},{9,10},{10,9},{11,... | collective-permute-start | bytes 18440 | tf_op jit(solution)/shard_map/ppermute | solution.py:358
  17.5 10.7 %collective-permute-start.1 = (f32[12,128]{1,0:T(8,128)S(1)}, f32[12,128]{1,0:T(8,128)S(1)}, u32[]{:S(2)}, u32[]{:S(2)}) collective-permute-start(f32[12,128]{1,0:T(8,128)S(1)} %shard_map.57), channel_id=1, source_target_pairs={{0,1},{1,0},{2,3},{3,2},{4,5},{5,4},{6,7},{7,6},{8,9},{9,8},{10,11... | collective-permute-start | bytes 18440 | tf_op jit(solution)/shard_map/ppermute | solution.py:374
  19.5 26.0 %collective-permute-start.2 = (f32[384,128]{1,0:T(8,128)S(1)}, f32[384,128]{1,0:T(8,128)S(1)}, u32[]{:S(2)}, u32[]{:S(2)}) collective-permute-start(f32[384,128]{1,0:T(8,128)S(1)} %shard_map.56.after_ref), channel_id=1, source_target_pairs={{32,64},{64,32},{96,128},{128,96},{160,192},{192,160},{224,256},{2... | collective-permute-start | bytes 589832 | tf_op jit(solution)/shard_map/ppermute | solution.py:368
  29.0 2.0 %copy-start.3 = (f32[1,1,256]{2,1,0:T(1,128)S(1)}, f32[1,1,256]{2,1,0:T(1,128)}, u32[]{:S(2)}) copy-start(f32[1,1,256]{2,1,0:T(1,128)} %param.7) | copy-start | bytes 3076
  29.0 2.0 %copy-start.2 = (f32[1,1,256]{2,1,0:T(1,128)S(1)}, f32[1,1,256]{2,1,0:T(1,128)}, u32[]{:S(2)}) copy-start(f32[1,1,256]{2,1,0:T(1,128)} %param.6) | copy-start | bytes 3076
  29.1 16.4 %collective-permute-start.4 = (f32[514,128]{1,0:T(8,128)S(1)}, f32[514,128]{1,0:T(8,128)S(1)}, u32[]{:S(2)}, u32[]{:S(2)}) collective-permute-start(f32[514,128]{1,0:T(8,128)S(1)} %shard_map.59), channel_id=1, source_target_pairs={{0,32},{32,0},{64,96},{96,64},{128,160},{160,128},{192,224},{224,1... | collective-permute-start | bytes 789512 | tf_op jit(solution)/shard_map/ppermute | solution.py:388
  31.0 14.4 %collective-permute-start.3 = (f32[130,128]{1,0:T(8,128)S(1)}, f32[130,128]{1,0:T(8,128)S(1)}, u32[]{:S(2)}, u32[]{:S(2)}) collective-permute-start(f32[130,128]{1,0:T(8,128)S(1)} %shard_map.58.after_ref), channel_id=1, source_target_pairs={{32,64},{64,32},{96,128},{128,96},{160,192},{192,160},{224,256},{2... | collective-permute-start | bytes 199688 | tf_op jit(solution)/shard_map/ppermute | solution.py:383
  38.4 0.7 copy-start.1

commit v7 on v6

--- a/solution.py
+++ b/solution.py
@@ -372,6 +372,7 @@
         compiler_params=params, cost_estimate=small,
     )(lon_flag, state, early)
     inner_edge = lax.ppermute(inner_edge, LON, lon_inner)
+    inner_edge, _ = lax.optimization_barrier((inner_edge, early))
     west = jnp.where(lon_even, outer_edge, inner_edge)
     east = jnp.where(lon_even, inner_edge, outer_edge)
 

time: 105 us -> 105 us (level)
    ppermute x1, starting transfers between devices: 1.92 us -> 4.03 us  [shards(): inner_edge = lax.ppermute(inner_edge, LON, lon_inner)]
    ppermute x1, starting transfers between devices: 16.2 us -> 14.5 us  [shards(): outer_edge = lax.ppermute(outer_edge, LON, lon_outer)]
where the time goes in v7:
time: 105 us
  blocking collectives  51.6 us (49%)
  starting transfers between devices  36.9 us (35%)
  Pallas kernels  7.23 us (7%)
  waiting for transfers between devices  5.92 us (6%)
  local copies, waits for them, and re-layouts  1.79 us (2%)
    all_to_all x1, blocking collectives, all_sum(): lax.all_to_all(block.reshape(plane, part, cols), PLANE, 0, 0, tiled=True)  21.4 us
    all_to_all x1, blocking collectives, all_sum(): lax.all_to_all(jnp.broadcast_to(mine[None], (line, part, cols)), LINE, 0,...  17.9 us
    ppermute x1, starting transfers between devices, shards(): outer_edge = lax.ppermute(outer_edge, LON, lon_outer)  14.5 us
    all_to_all x1, blocking collectives, all_sum(): lax.all_to_all(jnp.broadcast_to(mine[None], (plane, part, cols)), PLANE,...  12.3 us
    ppermute x1, starting transfers between devices, shards(): outer_early = lax.ppermute(early, LAT, outer_perm)  9.06 us
    ppermute x1, starting transfers between devices, shards(): outer_late = lax.ppermute(late, LAT, outer_perm)  7.37 us
    ppermute x1, waiting for transfers between devices, shards(): outer_late = lax.ppermute(late, LAT, outer_perm)  5.91 us
    pallas_call x1, Pallas kernels, shards(): pl.pallas_call(finish, out_shape=jax.ShapeDtypeStruct((entries, cols), jn...  5.64 us
  transfers between devices with their start and end apart: 5, of which 1 were waited for; matrix products, arithmetic and copies ran while one was open for 0% of the time, Pallas kernels for 0%

profile of v7, /device:TPU:1, one launch (start us, length us, event | category | flops | bytes accessed | tf_op | source)
XLA Modules:
  0.0 104.9 jit_solution(8056568731300103203)
XLA Ops:
  0.1 0.0 copy-start
  0.1 0.9 copy-done
  1.0 0.1 shard_map.55
  1.1 0.1 concatenate.3
  1.2 0.1 broadcast_in_dim.8.turn_ref
  1.4 4.0 %collective-permute-start.1 = (f32[12,128]{1,0:T(8,128)S(1)}, f32[12,128]{1,0:T(8,128)S(1)}, u32[]{:S(2)}, u32[]{:S(2)}) collective-permute-start(f32[12,128]{1,0:T(8,128)S(1)} %shard_map.57), channel_id=1, source_target_pairs={{0,1},{1,0},{2,3},{3,2},{4,5},{5,4},{6,7},{7,6},{8,9},{9,8},{10,11... | collective-permute-start | bytes 18440 | tf_op jit(solution)/shard_map/ppermute | solution.py:374
  5.4 14.5 %collective-permute-start = (f32[12,128]{1,0:T(8,128)S(1)}, f32[12,128]{1,0:T(8,128)S(1)}, u32[]{:S(2)}, u32[]{:S(2)}) collective-permute-start(f32[12,128]{1,0:T(8,128)S(1)} %get-tuple-element.12), channel_id=1, source_target_pairs={{1,2},{2,1},{3,4},{4,3},{5,6},{6,5},{7,8},{8,7},{9,10},{10,9},{11,... | collective-permute-start | bytes 18440 | tf_op jit(solution)/shard_map/ppermute | solution.py:358
  19.9 9.1 %collective-permute-start.2 = (f32[384,128]{1,0:T(8,128)S(1)}, f32[384,128]{1,0:T(8,128)S(1)}, u32[]{:S(2)}, u32[]{:S(2)}) collective-permute-start(f32[384,128]{1,0:T(8,128)S(1)} %shard_map.56.after_ref), channel_id=1, source_target_pairs={{32,64},{64,32},{96,128},{128,96},{160,192},{192,160},{224,256},{2... | collective-permute-start | bytes 589832 | tf_op jit(solution)/shard_map/ppermute | solution.py:368
  29.0 0.0 collective-permute-done.1
  29.0 0.0 collective-permute-done
  29.7 0.0 copy-start.3
  29.7 0.1 shard_map.59
  29.8 0.0 copy-start.2
  29.8 1.9 %collective-permute-start.4 = (f32[514,128]{1,0:T(8,128)S(1)}, f32[514,128]{1,0:T(8,128)S(1)}, u32[]{:S(2)}, u32[]{:S(2)}) collective-permute-start(f32[514,128]{1,0:T(8,128)S(1)} %shard_map.59), channel_id=1, source_target_pairs={{0,32},{32,0},{64,96},{96,64},{128,160},{160,128},{192,224},{224,1... | collective-permute-start | bytes 789512 | tf_op jit(solution)/shard_map/ppermute | solution.py:389
  31.7 0.0 copy-done.3
  31.7 0.0 copy-done.2
  31.8 7.4 %collective-permute-start.3 = (f32[130,128]{1,0:T(8,128)S(1)}, f32[130,128]{1,0:T(8,128)S(1)}, u32[]{:S(2)}, u32[]{:S(2)}) collective-permute-start(f32[130,128]{1,0:T(8,128)S(1)} %shard_map.58.after_ref), channel_id=1, source_target_pairs={{32,64},{64,32},{96,128},{128,96},{160,192},{192,160},{224,256},{2... | collective-permute-start | bytes 199688 | tf_op jit(solution)/shard_map/ppermute | solution.py:384
  39.1 0.0 copy-start.1
  39.1 0.7 copy-done.1
  39.8 0.5 fusion.weight_ref
  40.3 5.9 %collective-permute-done.3.late_ref = f32[130,128]{1,0:T(8,128)S(1)} collective-permute-done((f32[130,128]{1,0:T(8,128)S(1)}, f32[130,128]{1,0:T(8,128)S(1)}, u32[]{:S(2)}, u32[]{:S(2)}) %collective-permute-start.3) | collective-permute-done | bytes 66592 | tf_op jit(solution)/shard_map/ppermute | solution.py:384
  46.2 0.0 collective-permute-done.2.early_ref
  46.2 0.0 collective-permute-done.4.inner_ref
  46.2 1.3 %shard_map.60 = (f32[128,128]{1,0:T(8,128)S(1)}, f32[768,128]{1,0:T(8,128)S(1)}, f32[6,128]{1,0:T(8,128)S(1)}) custom-call(f32[8,128]{1,0:T(8,128)S(1)} %broadcast_in_dim.8.turn_ref, f32[768,128]{1,0:T(8,128)S(1)} %get-tuple-element.11.state_ref, f32[12,128]{1,0:T(8,128)S(1)} %get-tuple-element.20.west_ref, f32[12,128]{1,0:T(8,128)S(1)} %get-tuple-element.19.east_ref, ...), custom_call_target="tpu_custom_call" | custom-call | flops 30000000 | bytes 2000000 | tf_op jit(solution)/shard_map/pallas_call | solution.py:400
  47.5 21.4 %all_to_all.15 = f32[32,4,128]{2,1,0:T(4,128)S(1)} all-to-all(f32[32,4,128]{2,1,0:T(4,128)S(1)} %bitcast.17), channel_id=1, replica_groups=mesh['x'=4,'zh'=2,'core'=2,'zl'=8,'y'=4] {'x','core','y'}, dimensions={0} | all-to-all | bytes 131072 | tf_op jit(solution)/shard_map/all_to_all | solution.py:41
  68.9 17.9 %all_to_all.16 = f32[16,4,128]{2,1,0:T(4,128)S(1)} all-to-all(f32[16,4,128]{2,1,0:T(4,128)S(1)} %broadcast_in_dim.10), channel_id=1, replica_groups=mesh['x'=4,'zh'=2,'core'=2,'zl'=8,'y'=4] {'zh','zl'}, dimensions={0} | all-to-all | bytes 65536 | tf_op jit(solution)/shard_map/all_to_all | solution.py:42
  86.9 12.3 %all_to_all.17 = f32[32,4,128]{2,1,0:T(4,128)S(1)} all-to-all(f32[32,4,128]{2,1,0:T(4,128)S(1)} %broadcast_in_dim.11), channel_id=1, replica_groups=mesh['x'=4,'zh'=2,'core'=2,'zl'=8,'y'=4] {'x','core','y'}, dimensions={0} | all-to-all | bytes 131072 | tf_op jit(solution)/shard_map/all_to_all | solution.py:45
  99.2 5.6 %shard_map.61 = f32[768,128]{1,0:T(8,128)} custom-call(f32[128,128]{1,0:T(8,128)S(1)} %bitcast.15, f32[768,128]{1,0:T(8,128)S(1)} %get-tuple-element.15.x_ref, f32[6,128]{1,0:T(8,128)S(1)} %get-tuple-element.16.c_ref), custom_call_target="tpu_custom_call" | custom-call | flops 30000000 | bytes 1000000 | tf_op jit(solution)/shard_map/pallas_call | solution.py:416
  (11 shorter events, 0.2 us)
Async XLA Ops:
  0.1 0.9 copy-start
  1.4 27.6 %collective-permute-start.1 = (f32[12,128]{1,0:T(8,128)S(1)}, f32[12,128]{1,0:T(8,128)S(1)}, u32[]{:S(2)}, u32[]{:S(2)}) collective-permute-start(f32[12,128]{1,0:T(8,128)S(1)} %shard_map.57), channel_id=1, source_target_pairs={{0,1},{1,0},{2,3},{3,2},{4,5},{5,4},{6,7},{7,6},{8,9},{9,8},{10,11... | collective-permute-start | bytes 18440 | tf_op jit(solution)/shard_map/ppermute | solution.py:374
  5.4 23.6 %collective-permute-start = (f32[12,128]{1,0:T(8,128)S(1)}, f32[12,128]{1,0:T(8,128)S(1)}, u32[]{:S(2)}, u32[]{:S(2)}) collective-permute-start(f32[12,128]{1,0:T(8,128)S(1)} %get-tuple-element.12), channel_id=1, source_target_pairs={{1,2},{2,1},{3,4},{4,3},{5,6},{6,5},{7,8},{8,7},{9,10},{10,9},{11,... | collective-permute-start | bytes 18440 | tf_op jit(solution)/shard_map/ppermute | solution.py:358
  19.9 26.3 %collective-permute-start.2 = (f32[384,128]{1,0:T(8,128)S(1)}, f32[384,128]{1,0:T(8,128)S(1)}, u32[]{:S(2)}, u32[]{:S(2)}) collective-permute-start(f32[384,128]{1,0:T(8,128)S(1)} %shard_map.56.after_ref), channel_id=1, source_target_pairs={{32,64},{64,32},{96,128},{128,96},{160,192},{192,160},{224,256},{2... | collective-permute-start | bytes 589832 | tf_op jit(solution)/shard_map/ppermute | solution.py:368
  29.7 2.0 %copy-start.3 = (f32[1,1,256]{2,1,0:T(1,128)S(1)}, f32[1,1,256]{2,1,0:T(1,128)}, u32[]{:S(2)}) copy-start(f32[1,1,256]{2,1,0:T(1,128)} %param.7) | copy-start | bytes 3076
  29.8 2.0 %copy-start.2 = (f32[1,1,256]{2,1,0:T(1,128)S(1)}, f32[1,1,256]{2,1,0:T(1,128)}, u32[]{:S(2)}) copy-start(f32[1,1,256]{2,1,0:T(1,128)} %param.6) | copy-start | bytes 3076
  29.8 16.4 %collective-permute-start.4 = (f32[514,128]{1,0:T(8,128)S(1)}, f32[514,128]{1,0:T(8,128)S(1)}, u32[]{:S(2)}, u32[]{:S(2)}) collective-permute-start(f32[514,128]{1,0:T(8,128)S(1)} %shard_map.59), channel_id=1, source_target_pairs={{0,32},{32,0},{64,96},{96,64},{128,160},{160,128},{192,224},{224,1... | collective-permute-start | bytes 789512 | tf_op jit(solution)/shard_map/ppermute | solution.py:389
  31.8 14.4 %collective-permute-start.3 = (f32[130,128]{1,0:T(8,128)S(1)}, f32[130,128]{1,0:T(8,128)S(1)}, u32[]{:S(2)}, u32[]{:S(2)}) collective-permute-start(f32[130,128]{1,0:T(8,128)S(1)} %shard_map.58.after_ref), channel_id=1, source_target_pairs={{32,64},{64,32},{96,128},{128,96},{160,192},{192,160},{224,256},{2... | collective-permute-start | bytes 199688 | tf_op jit(solution)/shard_map/ppermute | solution.py:384
  39.1 0.7 copy-start.1
